TPU v7x, 256 devices: a whole 4x4x8 slice. The times are simulated.
256 devices in a mesh: gz: 4 (over z_hi, core), xy: 64 (over y, x, z_lo).
Axes of the slice: x: 4, y: 4, z: 8 (z_hi: 2, z_lo: 4; z = z_hi * 4 + z_lo), core: 2. Of those that a mesh axis runs over, the one named last changes fastest.
Arguments:
- left_vectors: float32 [3, 8, 16, 16, 64, 256], P(None, None, None, 'gz', 'xy'), may hold values from -6 to 6
- sign_seeds: int32 [16], replicated, may hold values from 0 to 16777215
- level_codes: int32 [16, 64, 256], P('gz', 'xy'), may hold values from 0 to 3
- level_table: float32 [4], replicated, may hold values from -1.5 to 1.5
- disorder_sites: int32 [4096], replicated, may hold values from 0 to 262143
- disorder_strength: float32 [4096], replicated, may hold values from -3 to 3
- hoppings: float32 [3, 8, 8], replicated, may hold values from -1.5 to 1.5
- mass_raw: float32 [8, 8], replicated, may hold values from -3 to 3
Outputs:
- moments: float32 [3, 4, 16], replicated
- cheb_prev: float32 [8, 16, 16, 64, 256], P(None, None, 'gz', 'xy')
- cheb_last: float32 [8, 16, 16, 64, 256], P(None, None, 'gz', 'xy')
All inputs are finite; a program needn't handle non-finite values.
Results may differ from a plain program's by a relative error of at most 0.0011.
Values may be sent and summed in bfloat16 or wider, within the bound.
A program may use at most 64 MiB of HBM per device.

v0:
```python
import functools
import math

import jax
import jax.numpy as jnp
from jax import lax
from jax.experimental import pallas as pl
from jax.experimental.pallas import tpu as pltpu
from jax.sharding import PartitionSpec as P

f32, bf16, i32 = jnp.float32, jnp.bfloat16, jnp.int32

PITCH = 24
NR = 608
LOHI = {0: (112, 496), 1: (80, 512), 2: (64, 544), 3: (32, 560)}
MULT = 668265261
NT = (((1,), (1,)), ((), ()))
highest = lax.Precision.HIGHEST


def split2(v):
    hi = v.astype(bf16)
    lo = (v - hi.astype(f32)).astype(bf16)
    return hi, lo


def split3(v):
    hi = v.astype(bf16)
    rest = v - hi.astype(f32)
    mid = rest.astype(bf16)
    lo = (rest - mid.astype(f32)).astype(bf16)
    return hi, mid, lo


def iota(shape, dim):
    return lax.broadcasted_iota(i32, shape, dim)


def rows_to_xy(rows):
    i = rows - 12
    q = lax.shift_right_arithmetic(i * 2731, jnp.full(i.shape, 16, i32))
    return q - 4, i - q * 24 - 4


def own_rows(block, lo):
    return jnp.concatenate(
        [block[112 + 24 * x - lo : 112 + 24 * x - lo + 16] for x in range(16)], axis=0
    )


def wrap32(value):
    value &= 0xFFFFFFFF
    return value - (1 << 32) if value >= (1 << 31) else value


def chain_kernel(
    place,
    seed_ref,
    hop_ref,
    mass_ref,
    on_ref,
    left_ref,
    prev_ref,
    last_ref,
    part_ref,
    wm_ref,
    wy_ref,
    w0_ref,
    wz_ref,
    hb_ref,
    mk_ref,
    sb_ref,
    f0_ref,
    f1_ref,
    f2_ref,
    a0_ref,
    a1_ref,
    a2_ref,
    b0_ref,
    b1_ref,
    b2_ref,
    c_ref,
    obc_ref,
    ob_ref,
    acc_ref,
):
    gz, tx, ty = place()

    lane8 = iota((8, 128), 1)
    spread = jnp.where(lax.shift_right_logical(lane8, 4) == iota((8, 128), 0), 1.0, 0.0)
    mass_raw = mass_ref[...]
    mass = 0.5 * (mass_raw + mass_raw.T)
    mats = [mass]
    for d in range(3):
        mats += [hop_ref[d].T, hop_ref[d]]
    stack = jnp.concatenate(mats, axis=0) * 0.4
    wide = jnp.dot(stack, spread, precision=highest, preferred_element_type=f32)
    same_r = (iota((16, 128), 1) & 15) == iota((16, 128), 0)
    full = []
    for k in range(7):
        blocks = []
        for b in range(8):
            row = wide[8 * k + b : 8 * k + b + 1]
            blocks.append(jnp.where(same_r, jnp.broadcast_to(row, (16, 128)), 0.0))
        full.append(split2(jnp.concatenate(blocks, axis=0)))
    for slot, k in enumerate((0, 1, 2, 5, 6)):
        both = jnp.concatenate(full[k], axis=1)
        wm_ref[256 * slot : 256 * slot + 128] = both
        wm_ref[256 * slot + 128 : 256 * slot + 256] = both
    for part in range(2):
        both = jnp.concatenate([full[3][part], full[4][part]], axis=1)
        wy_ref[256 * part : 256 * part + 128] = both
        wy_ref[256 * part + 128 : 256 * part + 256] = both
    w0_ref[0:128] = jnp.concatenate(full[1], axis=1)
    w0_ref[128:256] = -jnp.concatenate(full[2], axis=1)
    for part in range(2):
        wz_ref[128 * part : 128 * part + 128] = jnp.concatenate(
            [full[6][part], full[6][part], -full[5][part], -full[5][part]], axis=1
        )

    x, y = rows_to_xy(iota((576, 128), 0) + 8)
    lane = iota((576, 128), 1)
    xg = (tx * 16 + x + 128) & 127
    yg = ty * 16 + y
    lane1 = iota((1, 128), 1) & 15
    seeds = jnp.zeros((1, 128), i32)
    for r in range(16):
        seeds = jnp.where(lane1 == r, seed_ref[r], seeds)
    hb_ref[...] = ((xg * 128 + yg) * 8 + lax.shift_right_logical(lane, 4)) * MULT + seeds
    mk_ref[...] = jnp.where((yg >= 0) & (yg < 128), 1.0, 0.0)

    obc_ref[...] = jnp.zeros(obc_ref.shape, f32)
    for dx, h, lo, hi in ((0, 0, 96, 304), (0, 1, 288, 496), (-1, 1, 64, 112), (1, 0, 480, 544)):
        xr, yr = rows_to_xy(iota((hi - lo, 128), 0) + lo)
        xr = xr - 16 * dx - 8 * h
        ok = (xr >= 0) & (xr < 8)
        lane = iota((hi - lo, 128), 1)
        sels, vals = [], []
        for dy in (-1, 0, 1):
            yy = yr - 16 * dy
            hit = ok & (yy >= 0) & (yy < 16) & (xr * 16 + yy == lane)
            sel = jnp.where(hit, 1.0, 0.0).astype(bf16)
            for piece in split3(on_ref[(dx + 1) * 3 + dy + 1, h]):
                sels.append(sel)
                vals.append(piece)
        obc_ref[lo - 64 : hi - 64] += lax.dot_general(
            jnp.concatenate(sels, axis=1),
            jnp.concatenate(vals, axis=1),
            NT,
            preferred_element_type=f32,
        )
    for p in range(1, 11):
        col = (p // 4) * 8 + p % 4
        ob_ref[p - 1] = jnp.broadcast_to(obc_ref[:, col : col + 1] * 0.4, (480, 128))

    def sign_plane(p, carry):
        zg = (gz * 4 + p + 12) & 15
        word = hb_ref[...] + zg * wrap32(128 * 128 * 8 * MULT)
        word = word ^ lax.shift_right_logical(word, jnp.full(word.shape, 15, i32))
        word = word * -2048144789
        word = word ^ lax.shift_right_logical(word, jnp.full(word.shape, 13, i32))
        word = word * -1028477387
        mk = mk_ref[...]
        sb_ref[p] = jnp.where(word < 0, -mk, mk).astype(bf16)
        return carry

    lax.fori_loop(0, 12, sign_plane, 0)

    def keep(level, p, out, lo, hi):
        f_ref, a_ref, b_ref = ((f0_ref, a0_ref, b0_ref), (f1_ref, a1_ref, b1_ref), (f2_ref, a2_ref, b2_ref))[level]
        f_ref[p, lo:hi] = out
        hi_f = out.astype(bf16).astype(f32)
        lo_f = out - hi_f
        both = jnp.concatenate([hi_f, lo_f], axis=1)
        a_ref[p, lo:hi] = both.astype(bf16)
        b_ref[p, lo - 16 : hi] = jnp.concatenate([both[:8], both, both[:8]], axis=0).astype(bf16)
        return both

    def for_planes(level, radius, body):
        lo, hi = LOHI[radius]
        inner = functools.partial(body, lo=lo, hi=hi, own=True)
        lax.fori_loop(3, 9, lambda p, c: (inner(p), c)[1], 0)
        for k in range(1, radius + 1):
            lo, hi = LOHI[radius - k]
            outer = functools.partial(body, lo=lo, hi=hi, own=False)
            lax.fori_loop(0, 2, lambda i, c: (outer(3 - k + i * (5 + 2 * k)), c)[1], 0)

    def start(p, lo, hi, own):
        lhs = jnp.concatenate([sb_ref[p, lo + 16 : hi + 16], sb_ref[p, lo - 32 : hi - 32]], axis=1)
        prod = jnp.dot(lhs, w0_ref[...], preferred_element_type=f32)
        out = (prod[:, :128] + prod[:, 128:]) * 2.5
        both = keep(0, p, out, lo, hi)
        if own:
            c_ref[0, p - 3] = own_rows(both, lo).astype(bf16)

    for_planes(0, 3, start)

    fs = (f0_ref, f1_ref, f2_ref)
    as_ = (a0_ref, a1_ref, a2_ref)
    bs = (b0_ref, b1_ref, b2_ref)

    def step(n, p, lo, hi, own):
        a_ref, b_ref = as_[n], bs[n]
        lhs = jnp.concatenate(
            [
                a_ref[p, lo:hi],
                b_ref[p, lo + 16 : hi + 16],
                b_ref[p, lo - 32 : hi - 32],
                a_ref[p + 1, lo:hi],
                a_ref[p - 1, lo:hi],
            ],
            axis=1,
        )
        main = jnp.dot(lhs, wm_ref[...], preferred_element_type=f32)
        size = hi - lo + 16
        first = 0 if (lo, hi) == LOHI[1] else 16
        ylhs = a_ref[p, lo - first : lo - first + size]
        yy = jnp.dot(jnp.concatenate([ylhs, ylhs], axis=1), wy_ref[...], preferred_element_type=f32)
        yp = pltpu.roll(yy[:, :128], size - 1, 0)[first : first + hi - lo]
        ym = pltpu.roll(yy[:, 128:], 1, 0)[first : first + hi - lo]
        out = main[:, :128] + main[:, 128:] + yp + ym + ob_ref[p - 1, lo - 64 : hi - 64] * fs[n][p, lo:hi]
        out = out * mk_ref[lo - 8 : hi - 8]
        if n == 0:
            out = out * 0.5
        else:
            out = out - fs[n - 1][p, lo:hi]
        return out

    def step_keep(n, p, lo, hi, own):
        both = keep(n + 1, p, step(n, p, lo, hi, own), lo, hi)
        if own:
            c_ref[n + 1, p - 3] = own_rows(both, lo).astype(bf16)

    for_planes(1, 2, functools.partial(step_keep, 0))
    for_planes(2, 1, functools.partial(step_keep, 1))

    def step_last(p, lo, hi, own):
        out = step(2, p, lo, hi, own)
        v = own_rows(out, lo)
        hi_f = v.astype(bf16).astype(f32)
        c_ref[3, p - 3] = jnp.concatenate([hi_f, v - hi_f], axis=1).astype(bf16)
        f0_ref[p, 0:256] = v

    for_planes(3, 0, step_last)

    acc_ref[...] = jnp.zeros(acc_ref.shape, f32)

    def plane_out(z, carry):
        p = z + 4
        last = f0_ref[p, 0:256].T
        prev = own_rows(f2_ref[p, 80:512], 80).T
        for h in range(2):
            last_ref[pl.ds(2 * z + h, 128, stride=8), :] = last[:, 128 * h : 128 * h + 128]
            prev_ref[pl.ds(2 * z + h, 128, stride=8), :] = prev[:, 128 * h : 128 * h + 128]
        us = []
        for n in range(4):
            rhs = jnp.concatenate([c_ref[n, z + 2], c_ref[n, z]], axis=1)
            u = lax.dot_general(wz_ref[...], rhs, NT, preferred_element_type=f32)
            us.append(u[:128] + u[128:])
        for h in range(2):
            for m in range(3):
                lv = left_ref[m, pl.ds(2 * z + h, 128, stride=8), :]
                for n in range(4):
                    prod = lv * us[n][:, 128 * h : 128 * h + 128]
                    tot = prod[0:16]
                    for o in range(1, 8):
                        tot = tot + prod[16 * o : 16 * o + 16]
                    acc_ref[m * 4 + n] += tot
        return carry

    lax.fori_loop(0, 4, plane_out, 0)
    lanes = iota((8, 128), 1)
    part = jnp.zeros((8, 128), f32)
    for k in range(12):
        tot = jnp.sum(acc_ref[k], axis=1, keepdims=True)
        part = jnp.where(lanes == k, tot[0:8], part)
        part = jnp.where(lanes == k + 16, tot[8:16], part)
    part_ref[...] = part * (2.5 / math.sqrt(8 * 262144))


def chain(place, seeds, hoppings, mass_raw, on_halo, left):
    vm = pl.BlockSpec(memory_space=pltpu.VMEM)
    plane = lambda kind, lanes: pltpu.VMEM((12, NR, lanes), kind)
    return pl.pallas_call(
        functools.partial(chain_kernel, place),
        out_shape=(
            jax.ShapeDtypeStruct((1024, 128), f32),
            jax.ShapeDtypeStruct((1024, 128), f32),
            jax.ShapeDtypeStruct((8, 128), f32),
        ),
        in_specs=[pl.BlockSpec(memory_space=pltpu.SMEM), vm, vm, vm, vm],
        out_specs=(vm, vm, vm),
        scratch_shapes=[
            pltpu.VMEM((1280, 256), bf16),
            pltpu.VMEM((512, 256), bf16),
            pltpu.VMEM((256, 256), bf16),
            pltpu.VMEM((256, 512), bf16),
            pltpu.VMEM((576, 128), i32),
            pltpu.VMEM((576, 128), f32),
            pltpu.VMEM((12, 576, 128), bf16),
            plane(f32, 128),
            plane(f32, 128),
            plane(f32, 128),
            plane(bf16, 256),
            plane(bf16, 256),
            plane(bf16, 256),
            plane(bf16, 256),
            plane(bf16, 256),
            plane(bf16, 256),
            pltpu.VMEM((4, 6, 256, 256), bf16),
            pltpu.VMEM((480, 32), f32),
            pltpu.VMEM((10, 480, 128), f32),
            pltpu.VMEM((12, 16, 128), f32),
        ],
        compiler_params=pltpu.CompilerParams(vmem_limit_bytes=56 * 1024 * 1024),
        name="chain",
    )(seeds, hoppings, mass_raw, on_halo, left)


def where_am_i():
    tile = lax.axis_index("xy")
    return lax.axis_index("gz"), tile // 8, tile % 8


def onsite_kernel(codes_ref, table_ref, sites_ref, strength_ref, halo_ref, send_sem, recv_sem):
    gz, tx, ty = where_am_i()
    offsets = [(dx, dy, dz) for dx in (-1, 0, 1) for dy in (-1, 0, 1) for dz in (-1, 0, 1)]
    offsets = [o for o in offsets if o != (0, 0, 0)]

    def device(dx, dy, dz):
        tile = ((tx + dx + 8) % 8) * 8 + (ty + dy + 8) % 8
        return {"gz": (gz + dz + 4) % 4, "xy": tile}

    halo_ref[...] = jnp.zeros(halo_ref.shape, f32)
    barrier = pltpu.get_barrier_semaphore()
    for o in offsets:
        pl.semaphore_signal(barrier, inc=1, device_id=device(*o), device_id_type=pl.DeviceIdType.MESH)

    codes = codes_ref[...]
    base = jnp.zeros((8, 128), f32)
    for level in range(4):
        base = jnp.where(codes == level, table_ref[level], base)
    site = sites_ref[...]
    lz = (site >> 14) - gz * 4
    lx = ((site >> 7) & 127) - tx * 16
    ly = (site & 127) - ty * 16
    inside = (lz >= 0) & (lz < 4) & (lx >= 0) & (lx < 16) & (ly >= 0) & (ly < 16)
    row = jnp.where(inside, lz * 2 + (lx >> 3), -1)
    col = (lx & 7) * 16 + ly
    pieces = split3(strength_ref[...])
    lhs, rhs = [], []
    for k in range(32):
        hit = jnp.broadcast_to(row[k : k + 1], (8, 128)) == iota((8, 128), 0)
        lhs.append(
            jnp.concatenate(
                [jnp.where(hit, jnp.broadcast_to(p[k : k + 1].astype(f32), (8, 128)), 0.0) for p in pieces]
                + [jnp.zeros((8, 128), f32)],
                axis=0,
            ).astype(bf16)
        )
        at = jnp.broadcast_to(col[k : k + 1], (128, 128)) == iota((128, 128), 0)
        rhs.append(jnp.where(at, 1.0, 0.0).astype(bf16))
    added = lax.dot_general(
        jnp.concatenate(lhs, axis=1), jnp.concatenate(rhs, axis=1), NT, preferred_element_type=f32
    )
    onsite = base + (added[0:8] + added[8:16] + added[16:24])
    for z in range(4):
        for h in range(2):
            halo_ref[4, h, 8 + z : 9 + z] = onsite[2 * z + h : 2 * z + h + 1]

    pl.semaphore_wait(barrier, len(offsets))
    copies = []
    mine = halo_ref.at[4, :, pl.ds(8, 8)]
    for k, (dx, dy, dz) in enumerate(offsets):
        copy = pltpu.make_async_remote_copy(
            src_ref=mine,
            dst_ref=halo_ref.at[(1 - dx) * 3 + 1 - dy, :, pl.ds(8 * (1 - dz), 8)],
            send_sem=send_sem.at[k],
            recv_sem=recv_sem.at[k],
            device_id=device(dx, dy, dz),
            device_id_type=pl.DeviceIdType.MESH,
        )
        copy.start()
        copies.append(copy)
    for copy in copies:
        copy.wait()


def onsite_halo(level_codes, level_table, sites, strength):
    vm = pl.BlockSpec(memory_space=pltpu.VMEM)
    return pl.pallas_call(
        onsite_kernel,
        out_shape=jax.ShapeDtypeStruct((9, 2, 32, 128), f32),
        in_specs=[vm, pl.BlockSpec(memory_space=pltpu.SMEM), vm, vm],
        out_specs=vm,
        scratch_shapes=[pltpu.SemaphoreType.DMA((26,)), pltpu.SemaphoreType.DMA((26,))],
        compiler_params=pltpu.CompilerParams(
            collective_id=0, has_side_effects=True, vmem_limit_bytes=16 * 1024 * 1024
        ),
        name="onsite",
    )(level_codes, level_table, sites, strength)


def total_kernel(part_ref, out_ref, got_ref, mid_ref, send_sem, recv_sem):
    gz = lax.axis_index("gz")
    tile = lax.axis_index("xy")
    zpos = gz * 4 + tile % 4
    plane = tile // 4

    def along_z(step):
        other = (zpos + step) % 16
        return {"gz": other // 4, "xy": plane * 4 + other % 4}

    def along_plane(step):
        return {"gz": gz, "xy": ((plane + step) % 16) * 4 + tile % 4}

    barrier = pltpu.get_barrier_semaphore()
    for step in range(1, 16):
        for device in (along_z(step), along_plane(step)):
            pl.semaphore_signal(barrier, inc=1, device_id=device, device_id_type=pl.DeviceIdType.MESH)
    pl.semaphore_wait(barrier, 30)
    value = part_ref
    for stage, target in enumerate((along_z, along_plane)):
        copies = []
        for step in range(1, 16):
            copy = pltpu.make_async_remote_copy(
                src_ref=value,
                dst_ref=got_ref.at[stage, step - 1],
                send_sem=send_sem.at[stage, step - 1],
                recv_sem=recv_sem.at[stage, step - 1],
                device_id=target(step),
                device_id_type=pl.DeviceIdType.MESH,
            )
            copy.start()
            copies.append(copy)
        for copy in copies:
            copy.wait()
        total = value[...]
        for step in range(1, 16):
            total = total + got_ref[stage, step - 1]
        mid_ref[...] = total
        value = mid_ref
    flat = jnp.concatenate([total, jnp.zeros((120, 128), f32)], axis=0).T
    for m in range(3):
        out_ref[m, :, 0:8] = flat[4 * m : 4 * m + 4, 0:8]
        out_ref[m, :, 8:16] = flat[16 + 4 * m : 20 + 4 * m, 0:8]


def total(part):
    vm = pl.BlockSpec(memory_space=pltpu.VMEM)
    return pl.pallas_call(
        total_kernel,
        out_shape=jax.ShapeDtypeStruct((3, 4, 16), f32),
        in_specs=[vm],
        out_specs=vm,
        scratch_shapes=[
            pltpu.VMEM((2, 15, 8, 128), f32),
            pltpu.VMEM((8, 128), f32),
            pltpu.SemaphoreType.DMA((2, 15)),
            pltpu.SemaphoreType.DMA((2, 15)),
        ],
        compiler_params=pltpu.CompilerParams(
            collective_id=1, has_side_effects=True, vmem_limit_bytes=16 * 1024 * 1024
        ),
        name="total",
    )(part)


def per_device(
    left_vectors,
    sign_seeds,
    level_codes,
    level_table,
    disorder_sites,
    disorder_strength,
    hoppings,
    mass_raw,
):
    halo = onsite_halo(
        level_codes.reshape(8, 128),
        level_table,
        disorder_sites.reshape(32, 128),
        disorder_strength.reshape(32, 128),
    )
    prev, last, part = chain(
        where_am_i, sign_seeds, hoppings, mass_raw, halo, left_vectors.reshape(3, 1024, 128)
    )
    shape = left_vectors.shape[1:]
    return total(part), prev.reshape(shape), last.reshape(shape)


def solution(mesh):
    in_specs = (
        P(None, None, None, "gz", "xy", None),
        P(),
        P("gz", "xy", None),
        P(),
        P(),
        P(),
        P(),
        P(),
    )
    out_specs = (P(), P(None, None, "gz", "xy", None), P(None, None, "gz", "xy", None))
    return jax.shard_map(
        per_device, mesh=mesh, in_specs=in_specs, out_specs=out_specs, check_vma=False
    )
```

profile of v0, /device:TPU:1, one launch (start us, length us, event | category | flops | bytes accessed | tf_op | source)
XLA Modules:
  0.0 65.0 jit_solution(11027203475538261936)
XLA Ops:
  0.6 0.0 copy-start.1
  0.6 0.7 %copy-done.1 = s32[4096]{0:T(1024)S(1)} copy-done((s32[4096]{0:T(1024)S(1)}, s32[4096]{0:T(1024)}, u32[]{:S(2)}) %copy-start.1) | copy-done | bytes 16408
  1.4 0.0 copy-start.2
  1.4 0.7 %copy-done.2 = f32[4096]{0:T(1024)S(1)} copy-done((f32[4096]{0:T(1024)S(1)}, f32[4096]{0:T(1024)}, u32[]{:S(2)}) %copy-start.2) | copy-done | bytes 16408
  2.1 0.0 copy-start.4
  2.1 0.7 %copy-done.4 = s32[4,1,256]{2,1,0:T(1,128)S(1)} copy-done((s32[4,1,256]{2,1,0:T(1,128)S(1)}, s32[4,1,256]{2,1,0:T(1,128)}, u32[]{:S(2)}) %copy-start.4) | copy-done | bytes 4120
  2.8 0.0 copy-start.5
  2.8 0.7 %copy-done.5 = f32[4]{0:T(128)S(1)} copy-done((f32[4]{0:T(128)S(1)}, f32[4]{0:T(128)}, u32[]{:S(2)}) %copy-start.5) | copy-done | bytes 40
  3.4 21.4 %onsite.1.on_ref = f32[9,2,32,128]{3,2,1,0:T(8,128)S(1)} custom-call(s32[8,128]{1,0:T(8,128)S(1)} %bitcast.8, f32[4]{0:T(128)S(1)} %copy-done.5, s32[32,128]{1,0:T(8,128)S(1)} %bitcast.6, f32[32,128]{1,0:T(8,128)S(1)} %bitcast.7), custom_call_target="tpu_custom_call" | custom-call | tf_op jit(solution)/shard_map/onsite/pallas_call | solution.py:391
  24.8 0.0 copy-start
  24.9 0.7 %copy-done = f32[9,2,32,128]{3,2,1,0:T(8,128)} copy-done((f32[9,2,32,128]{3,2,1,0:T(8,128)}, f32[9,2,32,128]{3,2,1,0:T(8,128)S(1)}, u32[]{:S(2)}) %copy-start) | copy-done | bytes 294936
  25.6 24.4 %chain.1 = (f32[1024,128]{1,0:T(8,128)}, f32[1024,128]{1,0:T(8,128)}, f32[8,128]{1,0:T(8,128)}) custom-call(s32[16]{0:T(128)} %seed_ref.1, f32[3,8,8]{2,1,0:T(8,128)} %hop_ref.1, f32[8,8]{1,0:T(8,128)} %mass_ref.1, f32[9,2,32,128]{3,2,1,0:T(8,128)} %copy-done, f32[3,1024,128]{2,1,0:T(8,128)} %bitcast.9), custom_call_target="tpu_custom_call" | custom-call | tf_op jit(solution)/shard_map/chain/pallas_call | solution.py:284
  49.9 0.0 copy-start.3
  49.9 0.7 %copy-done.3 = f32[8,128]{1,0:T(8,128)S(1)} copy-done((f32[8,128]{1,0:T(8,128)S(1)}, f32[8,128]{1,0:T(8,128)}, u32[]{:S(2)}) %copy-start.3) | copy-done | bytes 4120
  50.6 13.7 %total.1 = f32[3,4,16]{2,1,0:T(4,128)S(1)} custom-call(f32[8,128]{1,0:T(8,128)S(1)} %copy-done.3), custom_call_target="tpu_custom_call" | custom-call | tf_op jit(solution)/shard_map/total/pallas_call | solution.py:451
  64.4 0.6 copy.14
Async XLA Ops:
  0.6 0.7 %copy-start.1 = (s32[4096]{0:T(1024)S(1)}, s32[4096]{0:T(1024)}, u32[]{:S(2)}) copy-start(s32[4096]{0:T(1024)} %param.12) | copy-start | bytes 49156
  1.4 0.7 %copy-start.2 = (f32[4096]{0:T(1024)S(1)}, f32[4096]{0:T(1024)}, u32[]{:S(2)}) copy-start(f32[4096]{0:T(1024)} %param.13) | copy-start | bytes 49156
  2.1 0.7 %copy-start.4 = (s32[4,1,256]{2,1,0:T(1,128)S(1)}, s32[4,1,256]{2,1,0:T(1,128)}, u32[]{:S(2)}) copy-start(s32[4,1,256]{2,1,0:T(1,128)} %param.10) | copy-start | bytes 12292
  2.8 0.7 %copy-start.5 = (f32[4]{0:T(128)S(1)}, f32[4]{0:T(128)}, u32[]{:S(2)}) copy-start(f32[4]{0:T(128)} %table_ref.1) | copy-start | bytes 52
  24.8 0.7 %copy-start = (f32[9,2,32,128]{3,2,1,0:T(8,128)}, f32[9,2,32,128]{3,2,1,0:T(8,128)S(1)}, u32[]{:S(2)}) copy-start(f32[9,2,32,128]{3,2,1,0:T(8,128)S(1)} %onsite.1.on_ref) | copy-start | bytes 884740
  49.9 0.7 %copy-start.3 = (f32[8,128]{1,0:T(8,128)S(1)}, f32[8,128]{1,0:T(8,128)}, u32[]{:S(2)}) copy-start(f32[8,128]{1,0:T(8,128)} %get-tuple-element.6.part_ref) | copy-start | bytes 12292
where the time goes:
time: 65.3 us; the launch traced here: 65 us
  Pallas kernels  59.6 us (91%)
  local copies, waits for them, and re-layouts  4.75 us (7%)
  between operations  0.67 us (1%)
    pallas_call x1, Pallas kernels, chain(): pl.pallas_call(functools.partial(chain_kernel, place), out_shape=(jax.Sha...  24.4 us
    pallas_call x1, Pallas kernels, onsite_halo(): pl.pallas_call(onsite_kernel, out_shape=jax.ShapeDtypeStruct((9, 2, 32, 1...  21.4 us
    pallas_call x1, Pallas kernels, total(): pl.pallas_call(total_kernel, out_shape=jax.ShapeDtypeStruct((3, 4, 16), f...  13.7 us
    unnamed x13, local copies, waits for them, and re-layouts  4.75 us

commit v1 on v0

v1 whole, which is shorter than its diff:
```python
import functools
import math

import jax
import jax.numpy as jnp
from jax import lax
from jax.experimental import pallas as pl
from jax.experimental.pallas import tpu as pltpu
from jax.sharding import PartitionSpec as P

f32, bf16, i32 = jnp.float32, jnp.bfloat16, jnp.int32

PITCH = 24
NR = 608
LOHI = {0: (112, 496), 1: (80, 512), 2: (64, 544), 3: (32, 560)}
MULT = 668265261
NT = (((1,), (1,)), ((), ()))
highest = lax.Precision.HIGHEST


def split2(v):
    hi = v.astype(bf16)
    lo = (v - hi.astype(f32)).astype(bf16)
    return hi, lo


def split3(v):
    hi = v.astype(bf16)
    rest = v - hi.astype(f32)
    mid = rest.astype(bf16)
    lo = (rest - mid.astype(f32)).astype(bf16)
    return hi, mid, lo


def iota(shape, dim):
    return lax.broadcasted_iota(i32, shape, dim)


def rows_to_xy(rows):
    i = rows - 12
    q = lax.shift_right_arithmetic(i * 2731, jnp.full(i.shape, 16, i32))
    return q - 4, i - q * 24 - 4


def own_rows(block, lo):
    return jnp.concatenate(
        [block[112 + 24 * x - lo : 112 + 24 * x - lo + 16] for x in range(16)], axis=0
    )


def wrap32(value):
    value &= 0xFFFFFFFF
    return value - (1 << 32) if value >= (1 << 31) else value


def groups_of(radius):
    sets = [(2, lambda i: [3 + 3 * i, 4 + 3 * i, 5 + 3 * i], LOHI[radius], True)]
    for k in range(1, radius + 1):
        sets.append((1, lambda i, k=k: [3 - k, 8 + k], LOHI[radius - k], False))
    return sets


def each_group(radius, body):
    for count, planes, (lo, hi), own in groups_of(radius):
        if count == 1:
            body(planes(0), lo, hi, own)
        else:
            lax.fori_loop(0, count, lambda i, c: (body(planes(i), lo, hi, own), c)[1], 0)


def rows(parts):
    return jnp.concatenate(parts, axis=0)


def lanes_of(parts):
    return jnp.concatenate(parts, axis=1)


def kernel(
    place,
    comm,
    seed_ref,
    hop_ref,
    mass_ref,
    codes_ref,
    table_ref,
    sites_ref,
    strength_ref,
    left_hbm,
    *refs,
):
    if not comm:
        halo_in, refs = refs[0], refs[1:]
    (
        moments_ref,
        prev_ref,
        last_ref,
        halo_ref,
        left_ref,
        wm_ref,
        wy_ref,
        w0_ref,
        wz_ref,
        hb_ref,
        mk_ref,
        sb_ref,
        f0_ref,
        f1_ref,
        f2_ref,
        a0_ref,
        a1_ref,
        a2_ref,
        b0_ref,
        b1_ref,
        b2_ref,
        c_ref,
        obc_ref,
        ob_ref,
        acc_ref,
        part_ref,
        got_ref,
        left_sem,
        send_sem,
        recv_sem,
        send2_sem,
        recv2_sem,
    ) = refs
    gz, tx, ty = place()
    load_left = pltpu.make_async_copy(left_hbm, left_ref, left_sem)
    load_left.start()

    halo_ref[...] = jnp.zeros(halo_ref.shape, f32)
    if comm:
        offsets = [(dx, dy, dz) for dx in (-1, 0, 1) for dy in (-1, 0, 1) for dz in (-1, 0, 1)]
        offsets = [o for o in offsets if o != (0, 0, 0)]

        def neighbour(dx, dy, dz):
            at = ((tx + dx + 8) % 8) * 8 + (ty + dy + 8) % 8
            return {"gz": (gz + dz + 4) % 4, "xy": at}

        tile = tx * 8 + ty
        zpos = gz * 4 + tile % 4
        column = tile // 4

        def along_z(step):
            other = (zpos + step) % 16
            return {"gz": other // 4, "xy": column * 4 + other % 4}

        def along_plane(step):
            return {"gz": gz, "xy": ((column + step) % 16) * 4 + tile % 4}

        barrier = pltpu.get_barrier_semaphore()
        partners = [neighbour(*o) for o in offsets]
        partners += [f(step) for f in (along_z, along_plane) for step in range(1, 16)]
        for device in partners:
            pl.semaphore_signal(barrier, inc=1, device_id=device, device_id_type=pl.DeviceIdType.MESH)

    codes = codes_ref[...]
    base = jnp.zeros((8, 128), f32)
    for level in range(4):
        base = jnp.where(codes == level, table_ref[level], base)
    site = sites_ref[...]
    lz = (site >> 14) - gz * 4
    lx = ((site >> 7) & 127) - tx * 16
    ly = (site & 127) - ty * 16
    inside = (lz >= 0) & (lz < 4) & (lx >= 0) & (lx < 16) & (ly >= 0) & (ly < 16)
    row = jnp.where(inside, lz * 2 + (lx >> 3), -1)
    col = (lx & 7) * 16 + ly
    pieces = split3(strength_ref[...])
    lhs, rhs = [], []
    for k in range(32):
        hit = jnp.broadcast_to(row[k : k + 1], (8, 128)) == iota((8, 128), 0)
        lhs.append(
            rows(
                [jnp.where(hit, jnp.broadcast_to(p[k : k + 1].astype(f32), (8, 128)), 0.0) for p in pieces]
                + [jnp.zeros((8, 128), f32)]
            ).astype(bf16)
        )
        at = jnp.broadcast_to(col[k : k + 1], (128, 128)) == iota((128, 128), 0)
        rhs.append(jnp.where(at, 1.0, 0.0).astype(bf16))
    added = lax.dot_general(lanes_of(lhs), lanes_of(rhs), NT, preferred_element_type=f32)
    onsite = base + (added[0:8] + added[8:16] + added[16:24])
    for z in range(4):
        for h in range(2):
            halo_ref[4, h, 8 + z : 9 + z] = onsite[2 * z + h : 2 * z + h + 1]

    spread = jnp.where(iota((8, 128), 1) >> 4 == iota((8, 128), 0), 1.0, 0.0)
    mass_raw = mass_ref[...]
    mass = 0.5 * (mass_raw + mass_raw.T)
    mats = [mass]
    for d in range(3):
        mats += [hop_ref[d].T, hop_ref[d]]
    wide = jnp.dot(rows(mats) * 0.4, spread, precision=highest, preferred_element_type=f32)
    same_r = (iota((16, 128), 1) & 15) == iota((16, 128), 0)
    full = []
    for k in range(7):
        blocks = []
        for b in range(8):
            row = wide[8 * k + b : 8 * k + b + 1]
            blocks.append(jnp.where(same_r, jnp.broadcast_to(row, (16, 128)), 0.0))
        full.append(split2(rows(blocks)))
    for slot, k in enumerate((0, 1, 2, 5, 6)):
        both = lanes_of(full[k])
        wm_ref[256 * slot : 256 * slot + 128] = both
        wm_ref[256 * slot + 128 : 256 * slot + 256] = both
    for part in range(2):
        both = lanes_of([full[3][part], full[4][part]])
        wy_ref[256 * part : 256 * part + 128] = both
        wy_ref[256 * part + 128 : 256 * part + 256] = both
    w0_ref[0:128] = lanes_of(full[1])
    w0_ref[128:256] = -lanes_of(full[2])
    for part in range(2):
        wz_ref[128 * part : 128 * part + 128] = lanes_of(
            [full[6][part], full[6][part], -full[5][part], -full[5][part]]
        )

    x, y = rows_to_xy(iota((576, 128), 0) + 8)
    lane = iota((576, 128), 1)
    xg = (tx * 16 + x + 128) & 127
    yg = ty * 16 + y
    lane1 = iota((1, 128), 1) & 15
    seeds = jnp.zeros((1, 128), i32)
    for r in range(16):
        seeds = jnp.where(lane1 == r, seed_ref[r], seeds)
    hb_ref[...] = ((xg * 128 + yg) * 8 + (lane >> 4)) * MULT + seeds
    mk_ref[...] = jnp.where((yg >= 0) & (yg < 128), 1.0, 0.0)

    def sign_plane(p, carry):
        zg = (gz * 4 + p + 12) & 15
        word = hb_ref[...] + zg * wrap32(128 * 128 * 8 * MULT)
        word = word ^ lax.shift_right_logical(word, jnp.full(word.shape, 15, i32))
        word = word * -2048144789
        word = word ^ lax.shift_right_logical(word, jnp.full(word.shape, 13, i32))
        word = word * -1028477387
        mk = mk_ref[...]
        sb_ref[p] = jnp.where(word < 0, -mk, mk).astype(bf16)
        return carry

    lax.fori_loop(0, 12, sign_plane, 0)

    fs = (f0_ref, f1_ref, f2_ref)
    as_ = (a0_ref, a1_ref, a2_ref)
    bs = (b0_ref, b1_ref, b2_ref)

    def keep(level, p, out, lo, hi, own):
        hi_f = out.astype(bf16).astype(f32)
        both = lanes_of([hi_f, out - hi_f])
        as_[level][p, lo:hi] = both.astype(bf16)
        bs[level][p, lo - 16 : hi] = rows([both[:8], both, both[:8]]).astype(bf16)
        if own:
            c_ref[level, p - 3] = own_rows(both, lo).astype(bf16)

    def start(planes, lo, hi, own):
        size = hi - lo
        lhs = rows([lanes_of([sb_ref[p, lo + 16 : hi + 16], sb_ref[p, lo - 32 : hi - 32]]) for p in planes])
        prod = jnp.dot(lhs, w0_ref[...], preferred_element_type=f32)
        prod = (prod[:, :128] + prod[:, 128:]) * 2.5
        for k, p in enumerate(planes):
            out = prod[k * size : k * size + size]
            f0_ref[p, lo:hi] = out
            keep(0, p, out, lo, hi, own)

    each_group(3, start)

    if comm:
        pl.semaphore_wait(barrier, len(partners))
        mine = halo_ref.at[4, :, pl.ds(8, 8)]
        sends = []
        for k, (dx, dy, dz) in enumerate(offsets):
            send = pltpu.make_async_remote_copy(
                src_ref=mine,
                dst_ref=halo_ref.at[(1 - dx) * 3 + 1 - dy, :, pl.ds(8 * (1 - dz), 8)],
                send_sem=send_sem.at[k],
                recv_sem=recv_sem.at[k],
                device_id=neighbour(dx, dy, dz),
                device_id_type=pl.DeviceIdType.MESH,
            )
            send.start()
            sends.append(send)

    def hop(n, planes, lo, hi):
        a_ref, b_ref = as_[n], bs[n]
        lhs = [
            lanes_of(
                [
                    a_ref[p, lo:hi],
                    b_ref[p, lo + 16 : hi + 16],
                    b_ref[p, lo - 32 : hi - 32],
                    a_ref[p + 1, lo:hi],
                    a_ref[p - 1, lo:hi],
                ]
            )
            for p in planes
        ]
        main = jnp.dot(rows(lhs), wm_ref[...], preferred_element_type=f32)
        size = hi - lo
        first = 0 if (lo, hi) == LOHI[1] else 16
        ylhs = rows([a_ref[p, lo - first : lo - first + size + 16] for p in planes])
        yy = jnp.dot(lanes_of([ylhs, ylhs]), wy_ref[...], preferred_element_type=f32)
        total = len(planes) * (size + 16)
        yp = pltpu.roll(yy[:, :128], total - 1, 0)
        ym = pltpu.roll(yy[:, 128:], 1, 0)
        outs = []
        for k in range(len(planes)):
            r, s = k * size, k * (size + 16) + first
            outs.append(main[r : r + size, :128] + main[r : r + size, 128:] + yp[s : s + size] + ym[s : s + size])
        return outs

    def first_hop(planes, lo, hi, own):
        for p, out in zip(planes, hop(0, planes, lo, hi)):
            f1_ref[p, lo:hi] = out

    each_group(2, first_hop)

    if comm:
        for send in sends:
            send.wait()
    else:
        halo_ref[...] = halo_in[...]
    obc_ref[...] = jnp.zeros(obc_ref.shape, f32)
    for dx, h, lo, hi in ((0, 0, 96, 304), (0, 1, 288, 496), (-1, 1, 64, 112), (1, 0, 480, 544)):
        xr, yr = rows_to_xy(iota((hi - lo, 128), 0) + lo)
        xr = xr - 16 * dx - 8 * h
        ok = (xr >= 0) & (xr < 8)
        lane = iota((hi - lo, 128), 1)
        sels, vals = [], []
        for dy in (-1, 0, 1):
            yy = yr - 16 * dy
            hit = ok & (yy >= 0) & (yy < 16) & (xr * 16 + yy == lane)
            sel = jnp.where(hit, 1.0, 0.0).astype(bf16)
            for piece in split3(halo_ref[(dx + 1) * 3 + dy + 1, h]):
                sels.append(sel)
                vals.append(piece)
        obc_ref[lo - 64 : hi - 64] += lax.dot_general(
            lanes_of(sels), lanes_of(vals), NT, preferred_element_type=f32
        )
    for p in range(1, 11):
        col = (p // 4) * 8 + p % 4
        ob_ref[p - 1] = jnp.broadcast_to(obc_ref[:, col : col + 1] * 0.4, (480, 128))

    def site_term(n, p, lo, hi):
        return ob_ref[p - 1, lo - 64 : hi - 64] * fs[n][p, lo:hi]

    def first_rest(planes, lo, hi, own):
        mask = mk_ref[lo - 8 : hi - 8] * 0.5
        for p in planes:
            out = (f1_ref[p, lo:hi] + site_term(0, p, lo, hi)) * mask
            f1_ref[p, lo:hi] = out
            keep(1, p, out, lo, hi, own)

    each_group(2, first_rest)

    def step(n, planes, lo, hi, own):
        mask = mk_ref[lo - 8 : hi - 8]
        for p, out in zip(planes, hop(n, planes, lo, hi)):
            out = (out + site_term(n, p, lo, hi)) * mask - fs[n - 1][p, lo:hi]
            if n == 1:
                f2_ref[p, lo:hi] = out
                keep(2, p, out, lo, hi, own)
            else:
                v = own_rows(out, lo)
                hi_f = v.astype(bf16).astype(f32)
                c_ref[3, p - 3] = lanes_of([hi_f, v - hi_f]).astype(bf16)
                f0_ref[p, 0:256] = v

    each_group(1, functools.partial(step, 1))
    each_group(0, functools.partial(step, 2))

    acc_ref[...] = jnp.zeros(acc_ref.shape, f32)
    load_left.wait()

    def plane_moments(z, carry):
        us = []
        for n in range(4):
            rhs = lanes_of([c_ref[n, z + 2], c_ref[n, z]])
            u = lax.dot_general(wz_ref[...], rhs, NT, preferred_element_type=f32)
            us.append(u[:128] + u[128:])
        for h in range(2):
            for m in range(3):
                lv = left_ref[m, pl.ds(2 * z + h, 128, stride=8), :]
                for n in range(4):
                    prod = lv * us[n][:, 128 * h : 128 * h + 128]
                    tot = prod[0:16]
                    for o in range(1, 8):
                        tot = tot + prod[16 * o : 16 * o + 16]
                    acc_ref[m * 4 + n] += tot
        return carry

    lax.fori_loop(0, 4, plane_moments, 0)
    lanes = iota((8, 128), 1)
    part = jnp.zeros((8, 128), f32)
    for k in range(12):
        tot = jnp.sum(acc_ref[k], axis=1, keepdims=True)
        part = jnp.where(lanes == k, tot[0:8], part)
        part = jnp.where(lanes == k + 16, tot[8:16], part)
    part = part * (2.5 / math.sqrt(8 * 262144))
    part_ref[0] = part

    def send_part(stage, target):
        copies = []
        for step in range(1, 16):
            copy = pltpu.make_async_remote_copy(
                src_ref=part_ref.at[stage],
                dst_ref=got_ref.at[stage, step - 1],
                send_sem=send2_sem.at[stage, step - 1],
                recv_sem=recv2_sem.at[stage, step - 1],
                device_id=target(step),
                device_id_type=pl.DeviceIdType.MESH,
            )
            copy.start()
            copies.append(copy)
        return copies

    def add_parts(stage, copies, total):
        for copy in copies:
            copy.wait()
        for step in range(1, 16):
            total = total + got_ref[stage, step - 1]
        return total

    if comm:
        copies = send_part(0, along_z)

    def plane_out(z, carry):
        last = f0_ref[z + 4, 0:256].T
        prev = own_rows(f2_ref[z + 4, 80:512], 80).T
        for h in range(2):
            last_ref[pl.ds(2 * z + h, 128, stride=8), :] = last[:, 128 * h : 128 * h + 128]
            prev_ref[pl.ds(2 * z + h, 128, stride=8), :] = prev[:, 128 * h : 128 * h + 128]
        return carry

    lax.fori_loop(0, 4, plane_out, 0)

    if comm:
        part = add_parts(0, copies, part)
        part_ref[1] = part
        part = add_parts(1, send_part(1, along_plane), part)
    flat = rows([part, jnp.zeros((120, 128), f32)]).T
    for m in range(3):
        moments_ref[m, :, 0:8] = flat[4 * m : 4 * m + 4, 0:8]
        moments_ref[m, :, 8:16] = flat[16 + 4 * m : 20 + 4 * m, 0:8]


def whole(place, comm, seeds, hoppings, mass_raw, codes, table, sites, strength, left, *halo):
    vm = pl.BlockSpec(memory_space=pltpu.VMEM)
    sm = pl.BlockSpec(memory_space=pltpu.SMEM)
    plane = lambda kind, lanes: pltpu.VMEM((12, NR, lanes), kind)
    dma = pltpu.SemaphoreType.DMA
    extra = {"collective_id": 0, "has_side_effects": True} if comm else {}
    return pl.pallas_call(
        functools.partial(kernel, place, comm),
        out_shape=(
            jax.ShapeDtypeStruct((3, 4, 16), f32),
            jax.ShapeDtypeStruct((1024, 128), f32),
            jax.ShapeDtypeStruct((1024, 128), f32),
        ),
        in_specs=[sm, vm, vm, vm, sm, vm, vm, pl.BlockSpec(memory_space=pl.ANY)] + [vm] * len(halo),
        out_specs=(vm, vm, vm),
        scratch_shapes=[
            pltpu.VMEM((9, 2, 32, 128), f32),
            pltpu.VMEM((3, 1024, 128), f32),
            pltpu.VMEM((1280, 256), bf16),
            pltpu.VMEM((512, 256), bf16),
            pltpu.VMEM((256, 256), bf16),
            pltpu.VMEM((256, 512), bf16),
            pltpu.VMEM((576, 128), i32),
            pltpu.VMEM((576, 128), f32),
            pltpu.VMEM((12, 576, 128), bf16),
            plane(f32, 128),
            plane(f32, 128),
            plane(f32, 128),
            plane(bf16, 256),
            plane(bf16, 256),
            plane(bf16, 256),
            plane(bf16, 256),
            plane(bf16, 256),
            plane(bf16, 256),
            pltpu.VMEM((4, 6, 256, 256), bf16),
            pltpu.VMEM((480, 32), f32),
            pltpu.VMEM((10, 480, 128), f32),
            pltpu.VMEM((12, 16, 128), f32),
            pltpu.VMEM((2, 8, 128), f32),
            pltpu.VMEM((2, 15, 8, 128), f32),
            dma,
            dma((26,)),
            dma((26,)),
            dma((2, 15)),
            dma((2, 15)),
        ],
        compiler_params=pltpu.CompilerParams(vmem_limit_bytes=60 * 1024 * 1024, **extra),
        name="chain",
    )(seeds, hoppings, mass_raw, codes, table, sites, strength, left, *halo)


def where_am_i():
    tile = lax.axis_index("xy")
    return lax.axis_index("gz"), tile // 8, tile % 8


def per_device(
    left_vectors,
    sign_seeds,
    level_codes,
    level_table,
    disorder_sites,
    disorder_strength,
    hoppings,
    mass_raw,
):
    moments, prev, last = whole(
        where_am_i,
        True,
        sign_seeds,
        hoppings,
        mass_raw,
        level_codes.reshape(8, 128),
        level_table,
        disorder_sites.reshape(32, 128),
        disorder_strength.reshape(32, 128),
        left_vectors.reshape(3, 1024, 128),
    )
    shape = left_vectors.shape[1:]
    return moments, prev.reshape(shape), last.reshape(shape)


def solution(mesh):
    in_specs = (
        P(None, None, None, "gz", "xy", None),
        P(),
        P("gz", "xy", None),
        P(),
        P(),
        P(),
        P(),
        P(),
    )
    out_specs = (P(), P(None, None, "gz", "xy", None), P(None, None, "gz", "xy", None))
    return jax.shard_map(
        per_device, mesh=mesh, in_specs=in_specs, out_specs=out_specs, check_vma=False
    )
```

time: 65.3 us -> 50.5 us (0.77)
  Pallas kernels: 59.6 us -> 43.9 us
  local copies, waits for them, and re-layouts: 4.75 us -> 5.67 us
    pallas_call x3 -> x1, Pallas kernels: 59.6 us -> 43.9 us  [whole(): pl.pallas_call(functools.partial(kernel, place, comm), out_shape=(jax.Sha...]
    unnamed x13 -> x3, local copies, waits for them, and re-layouts: 4.75 us -> 5.67 us
where the time goes in v1:
time: 50.5 us; the launch traced here: 50.2 us
  Pallas kernels  43.9 us (87%)
  local copies, waits for them, and re-layouts  5.67 us (11%)
  between operations  0.64 us (1%)
    pallas_call x1, Pallas kernels, whole(): pl.pallas_call(functools.partial(kernel, place, comm), out_shape=(jax.Sha...  43.9 us
    unnamed x3, local copies, waits for them, and re-layouts  5.67 us

profile of v1, /device:TPU:1, one launch (start us, length us, event | category | flops | bytes accessed | tf_op | source)
XLA Modules:
  0.0 50.2 jit_solution(132468985449189445)
XLA Ops:
  0.6 43.9 %chain.1 = (f32[3,4,16]{2,1,0:T(4,128)}, f32[1024,128]{1,0:T(8,128)}, f32[1024,128]{1,0:T(8,128)}) custom-call(s32[16]{0:T(128)} %seed_ref.1, f32[3,8,8]{2,1,0:T(8,128)} %hop_ref.1, f32[8,8]{1,0:T(8,128)} %mass_ref.1, s32[8,128]{1,0:T(8,128)} %bitcast.11, f32[4]{0:T(128)} %table_ref.1, s32[32,128]{1,0:T(8,128)} %bitcast.9, f32[32,128]{1,0:T(8,128)} %bitcast.10, ...), custom_call_target="tpu_custom_call" | custom-call | tf_op jit(solution)/shard_map/chain/pallas_call | solution.py:450
  44.5 1.3 %copy.16 = f32[3,4,16]{2,1,0:T(4,128)} copy(f32[3,4,16]{2,1,0:T(4,128)} %get-tuple-element.15) | data formatting | bytes 1536
  45.8 2.2 %copy.17 = f32[8,16,4,1,256]{4,3,2,1,0:T(1,128)} copy(f32[8,16,4,1,256]{4,3,2,1,0:T(1,128)} %bitcast.8) | data formatting | bytes 1048576
  48.0 2.2 %copy.18 = f32[8,16,4,1,256]{4,3,2,1,0:T(1,128)} copy(f32[8,16,4,1,256]{4,3,2,1,0:T(1,128)} %bitcast.7) | data formatting | bytes 1048576

commit v2 on v1

v2 whole, which is shorter than its diff:
```python
import functools
import math

import jax
import jax.numpy as jnp
from jax import lax
from jax.experimental import pallas as pl
from jax.experimental.pallas import tpu as pltpu
from jax.sharding import PartitionSpec as P

f32, bf16, i32 = jnp.float32, jnp.bfloat16, jnp.int32

PITCH = 24
NR = 608
LOHI = {0: (112, 496), 1: (80, 512), 2: (64, 544), 3: (32, 560)}
MULT = 668265261
NT = (((1,), (1,)), ((), ()))
highest = lax.Precision.HIGHEST


def split2(v):
    hi = v.astype(bf16)
    lo = (v - hi.astype(f32)).astype(bf16)
    return hi, lo


def split3(v):
    hi = v.astype(bf16)
    rest = v - hi.astype(f32)
    mid = rest.astype(bf16)
    lo = (rest - mid.astype(f32)).astype(bf16)
    return hi, mid, lo


def iota(shape, dim):
    return lax.broadcasted_iota(i32, shape, dim)


def rows_to_xy(rows):
    i = rows - 12
    q = lax.shift_right_arithmetic(i * 2731, jnp.full(i.shape, 16, i32))
    return q - 4, i - q * 24 - 4


def own_rows(block, lo):
    return jnp.concatenate(
        [block[112 + 24 * x - lo : 112 + 24 * x - lo + 16] for x in range(16)], axis=0
    )


def wrap32(value):
    value &= 0xFFFFFFFF
    return value - (1 << 32) if value >= (1 << 31) else value


def rows(parts):
    return jnp.concatenate(parts, axis=0)


def lanes_of(parts):
    return jnp.concatenate(parts, axis=1)


MESH = pl.DeviceIdType.MESH
SEGMENTS = ((0, 0, 96, 304), (0, 1, 288, 496), (-1, 1, 64, 112), (1, 0, 480, 544))


def kernel(
    place,
    comm,
    seed_hbm,
    hop_hbm,
    mass_hbm,
    codes_hbm,
    table_hbm,
    sites_hbm,
    strength_hbm,
    left_hbm,
    *refs,
):
    if not comm:
        (halo_in, a1_in, a2_in, c_in), refs = refs[:4], refs[4:]
    (
        moments_ref,
        prev_ref,
        last_ref,
        seed_ref,
        hop_ref,
        mass_ref,
        codes_ref,
        table_ref,
        sites_ref,
        strength_ref,
        left_ref,
        halo_ref,
        wm_ref,
        wy_ref,
        w0_ref,
        wz_ref,
        hb_ref,
        mk_ref,
        sb_ref,
        f0_ref,
        f1_ref,
        f2_ref,
        a0_ref,
        a1_ref,
        a2_ref,
        b0_ref,
        b1_ref,
        b2_ref,
        c_ref,
        sel_ref,
        obc_ref,
        ob_ref,
        acc_ref,
        part_ref,
        got_ref,
        load_sem,
        send_sem,
        recv_sem,
        pair_send_sem,
        pair_recv_sem,
        send2_sem,
        recv2_sem,
    ) = refs
    gz, tx, ty = place()
    odd = gz % 2 == 1
    flip = gz % 2 * 2 - 1

    def z_of(p):
        return (3 * (1 - gz % 2)) + flip * (p - 1)

    if comm:
        near = [(dx, dy) for dx in (-1, 0, 1) for dy in (-1, 0, 1) if (dx, dy) != (0, 0)]
        outer = (gz + flip + 4) % 4
        inner = (gz - flip + 4) % 4
        tile = tx * 8 + ty
        zpos = gz * 4 + tile % 4
        column = tile // 4

        def neighbour(dx, dy, z):
            return {"gz": z, "xy": ((tx + dx + 8) % 8) * 8 + (ty + dy + 8) % 8}

        def along_z(step):
            other = (zpos + step) % 16
            return {"gz": other // 4, "xy": column * 4 + other % 4}

        def along_plane(step):
            return {"gz": gz, "xy": ((column + step) % 16) * 4 + tile % 4}

        barrier = pltpu.get_barrier_semaphore()
        partners = [neighbour(dx, dy, outer) for dx, dy in near]
        partners += [neighbour(dx, dy, gz) for dx, dy in near]
        partners += [f(step) for f in (along_z, along_plane) for step in range(1, 16)]
        for device in partners:
            pl.semaphore_signal(barrier, inc=1, device_id=device, device_id_type=MESH)

    loads = []
    for k, (src, dst) in enumerate(
        (
            (sites_hbm, sites_ref),
            (strength_hbm, strength_ref),
            (codes_hbm, codes_ref),
            (table_hbm, table_ref),
            (hop_hbm, hop_ref),
            (mass_hbm, mass_ref),
            (seed_hbm, seed_ref),
            (left_hbm, left_ref),
        )
    ):
        loads.append(pltpu.make_async_copy(src, dst, load_sem.at[k]))
        loads[-1].start()

    for load in loads[:4]:
        load.wait()
    codes = codes_ref[...]
    base = jnp.zeros((8, 128), f32)
    for level in range(4):
        base = jnp.where(codes == level, table_ref[level], base)
    site = sites_ref[...]
    lz = (site >> 14) - gz * 4
    lx = ((site >> 7) & 127) - tx * 16
    ly = (site & 127) - ty * 16
    inside = (lz >= 0) & (lz < 4) & (lx >= 0) & (lx < 16) & (ly >= 0) & (ly < 16)
    row = jnp.where(inside, lz * 2 + (lx >> 3), -1)
    col = (lx & 7) * 16 + ly
    pieces = split3(strength_ref[...])
    lhs, rhs = [], []
    for k in range(32):
        hit = jnp.broadcast_to(row[k : k + 1], (8, 128)) == iota((8, 128), 0)
        lhs.append(
            rows(
                [jnp.where(hit, jnp.broadcast_to(p[k : k + 1].astype(f32), (8, 128)), 0.0) for p in pieces]
                + [jnp.zeros((8, 128), f32)]
            ).astype(bf16)
        )
        at = jnp.broadcast_to(col[k : k + 1], (128, 128)) == iota((128, 128), 0)
        rhs.append(jnp.where(at, 1.0, 0.0).astype(bf16))
    added = lax.dot_general(lanes_of(lhs), lanes_of(rhs), NT, preferred_element_type=f32)
    onsite = base + (added[0:8] + added[8:16] + added[16:24])
    for h in range(2):
        up = [onsite[2 * z + h : 2 * z + h + 1] for z in range(4)]
        block = jnp.where(odd, rows(up), rows(up[::-1]))
        halo_ref[0, 4, h] = rows([block, jnp.zeros((4, 128), f32)])

    if comm:
        pl.semaphore_wait(barrier, len(partners))
        near_sends, far_sends = [], []
        for k, (dx, dy, far) in enumerate(
            [(dx, dy, True) for dx, dy in near] + [(0, 0, True)] + [(dx, dy, False) for dx, dy in near]
        ):
            send = pltpu.make_async_remote_copy(
                src_ref=halo_ref.at[0, 4],
                dst_ref=halo_ref.at[int(far), (1 - dx) * 3 + 1 - dy],
                send_sem=send_sem.at[k],
                recv_sem=recv_sem.at[k],
                device_id=neighbour(dx, dy, outer if far else gz),
                device_id_type=MESH,
            )
            send.start()
            (far_sends if far else near_sends).append(send)

    for load in loads[4:7]:
        load.wait()
    spread = jnp.where(iota((8, 128), 1) >> 4 == iota((8, 128), 0), 1.0, 0.0)
    mass_raw = mass_ref[...]
    mats = [0.5 * (mass_raw + mass_raw.T)]
    for d in range(3):
        mats += [hop_ref[d].T, hop_ref[d]]
    wide = jnp.dot(rows(mats) * 0.4, spread, precision=highest, preferred_element_type=f32)
    wide = [wide[8 * k : 8 * k + 8] for k in range(7)]
    same_r = (iota((16, 128), 1) & 15) == iota((16, 128), 0)

    def matrix(narrow):
        blocks = [jnp.where(same_r, jnp.broadcast_to(narrow[b : b + 1], (16, 128)), 0.0) for b in range(8)]
        return split2(rows(blocks))

    w_mass, w_xp, w_xm, w_yp, w_ym = [matrix(w) for w in wide[:5]]
    w_next = matrix(jnp.where(odd, wide[5], wide[6]))
    w_before = matrix(jnp.where(odd, wide[6], wide[5]))
    v_next = matrix(jnp.where(odd, wide[6], -wide[5]))
    v_before = matrix(jnp.where(odd, -wide[5], wide[6]))
    for slot, pair in enumerate((w_mass, w_xp, w_xm, w_next, w_before)):
        both = lanes_of(pair)
        wm_ref[256 * slot : 256 * slot + 128] = both
        wm_ref[256 * slot + 128 : 256 * slot + 256] = both
    for part in range(2):
        both = lanes_of([w_yp[part], w_ym[part]])
        wy_ref[256 * part : 256 * part + 128] = both
        wy_ref[256 * part + 128 : 256 * part + 256] = both
        wz_ref[128 * part : 128 * part + 128] = lanes_of([v_next[part]] * 2 + [v_before[part]] * 2)
    w0_ref[0:128] = lanes_of(w_xp)
    w0_ref[128:256] = -lanes_of(w_xm)

    x, y = rows_to_xy(iota((576, 128), 0) + 8)
    lane = iota((576, 128), 1)
    xg = (tx * 16 + x + 128) & 127
    yg = ty * 16 + y
    lane1 = iota((1, 128), 1) & 15
    seeds = jnp.zeros((1, 128), i32)
    for r in range(16):
        seeds = jnp.where(lane1 == r, seed_ref[r], seeds)
    hb_ref[...] = ((xg * 128 + yg) * 8 + (lane >> 4)) * MULT + seeds
    mk_ref[...] = jnp.where((yg >= 0) & (yg < 128), 1.0, 0.0)

    def sign_plane(p, carry):
        zg = (gz * 4 + z_of(p) + 16) & 15
        word = hb_ref[...] + zg * wrap32(128 * 128 * 8 * MULT)
        word = word ^ lax.shift_right_logical(word, jnp.full(word.shape, 15, i32))
        word = word * -2048144789
        word = word ^ lax.shift_right_logical(word, jnp.full(word.shape, 13, i32))
        word = word * -1028477387
        mk = mk_ref[...]
        sb_ref[p] = jnp.where(word < 0, -mk, mk).astype(bf16)
        return carry

    lax.fori_loop(0, 9, sign_plane, 0)

    at = 0
    for dx, h, lo, hi in SEGMENTS:
        xr, yr = rows_to_xy(iota((hi - lo, 128), 0) + lo)
        xr = xr - 16 * dx - 8 * h
        ok = (xr >= 0) & (xr < 8)
        lane = iota((hi - lo, 128), 1)
        sels = []
        for dy in (-1, 0, 1):
            yy = yr - 16 * dy
            hit = ok & (yy >= 0) & (yy < 16) & (xr * 16 + yy == lane)
            sels.append(jnp.where(hit, 1.0, 0.0).astype(bf16))
        sel_ref[at : at + hi - lo] = lanes_of(sels)
        at += hi - lo

    fs = (f0_ref, f1_ref, f2_ref)
    as_ = (a0_ref, a1_ref, a2_ref)
    bs = (b0_ref, b1_ref, b2_ref)

    def keep(level, p, out, lo, hi):
        hi_f = out.astype(bf16).astype(f32)
        both = lanes_of([hi_f, out - hi_f])
        as_[level][p, lo:hi] = both.astype(bf16)
        bs[level][p, lo - 16 : hi] = rows([both[:8], both, both[:8]]).astype(bf16)
        if p <= 5:
            c_ref[level, p] = own_rows(both, lo).astype(bf16)

    def start(planes):
        lhs = []
        for p, radius in planes:
            lo, hi = LOHI[radius]
            lhs.append(lanes_of([sb_ref[p, lo + 16 : hi + 16], sb_ref[p, lo - 32 : hi - 32]]))
        prod = jnp.dot(rows(lhs), w0_ref[...], preferred_element_type=f32)
        prod = (prod[:, :128] + prod[:, 128:]) * 2.5
        at = 0
        for p, radius in planes:
            lo, hi = LOHI[radius]
            out = prod[at : at + hi - lo]
            at += hi - lo
            f0_ref[p, lo:hi] = out
            keep(0, p, out, lo, hi)

    start(((0, 2), (1, 3), (2, 3)))
    start(((3, 3), (4, 3), (5, 3)))
    start(((6, 2), (7, 1), (8, 0)))

    def hop(n, planes):
        a_ref, b_ref = as_[n], bs[n]
        lhs, ylhs = [], []
        for p, radius in planes:
            lo, hi = LOHI[radius]
            lhs.append(
                lanes_of(
                    [
                        a_ref[p, lo:hi],
                        b_ref[p, lo + 16 : hi + 16],
                        b_ref[p, lo - 32 : hi - 32],
                        a_ref[p + 1, lo:hi],
                        a_ref[p - 1, lo:hi],
                    ]
                )
            )
            first = 0 if radius == 1 else 16
            ylhs.append(a_ref[p, lo - first : hi + 16 - first])
        main = jnp.dot(rows(lhs), wm_ref[...], preferred_element_type=f32)
        ylhs = rows(ylhs)
        yy = jnp.dot(lanes_of([ylhs, ylhs]), wy_ref[...], preferred_element_type=f32)
        yp = pltpu.roll(yy[:, :128], yy.shape[0] - 1, 0)
        ym = pltpu.roll(yy[:, 128:], 1, 0)
        outs, r, s = [], 0, 0
        for p, radius in planes:
            lo, hi = LOHI[radius]
            first = 0 if radius == 1 else 16
            size, t = hi - lo, s + first
            outs.append(main[r : r + size, :128] + main[r : r + size, 128:] + yp[t : t + size] + ym[t : t + size])
            r += size
            s += size + 16
        return outs

    def first_hop(planes):
        for (p, radius), out in zip(planes, hop(0, planes)):
            lo, hi = LOHI[radius]
            f1_ref[p, lo:hi] = out

    first_hop(((1, 2), (2, 2), (3, 2)))
    first_hop(((4, 2), (5, 2), (6, 1), (7, 0)))

    def energies(far, planes):
        obc_ref[...] = jnp.zeros(obc_ref.shape, f32)
        at = 0
        for dx, h, lo, hi in SEGMENTS:
            sels, vals = [], []
            for dy in (-1, 0, 1):
                sel = sel_ref[at : at + hi - lo, 128 * (dy + 1) : 128 * (dy + 2)]
                block = halo_ref[far, (dx + 1) * 3 + dy + 1, h]
                for piece in split3(rows([block, jnp.zeros((8, 128), f32)])):
                    sels.append(sel)
                    vals.append(piece)
            at += hi - lo
            obc_ref[lo - 64 : hi - 64] += lax.dot_general(
                lanes_of(sels), lanes_of(vals), NT, preferred_element_type=f32
            )
        for p, col in planes:
            ob_ref[p] = jnp.broadcast_to(obc_ref[:, col : col + 1] * 0.4, (480, 128))

    def site_term(n, p, lo, hi):
        return ob_ref[p, lo - 64 : hi - 64] * fs[n][p, lo:hi]

    def first_rest(planes):
        for p, radius in planes:
            lo, hi = LOHI[radius]
            out = (f1_ref[p, lo:hi] + site_term(0, p, lo, hi)) * (mk_ref[lo - 8 : hi - 8] * 0.5)
            f1_ref[p, lo:hi] = out
            keep(1, p, out, lo, hi)

    def step(n, planes):
        for (p, radius), out in zip(planes, hop(n, planes)):
            lo, hi = LOHI[radius]
            out = (out + site_term(n, p, lo, hi)) * mk_ref[lo - 8 : hi - 8] - fs[n - 1][p, lo:hi]
            if n == 1:
                f2_ref[p, lo:hi] = out
                keep(2, p, out, lo, hi)
            else:
                v = own_rows(out, lo)
                hi_f = v.astype(bf16).astype(f32)
                c_ref[3, p] = lanes_of([hi_f, v - hi_f]).astype(bf16)
                f0_ref[p, 0:256] = v

    pair_sends = []

    def to_pair(level):
        if not comm:
            if level < 3:
                as_[level][0] = (a1_in, a2_in)[level - 1][...]
            c_ref[level, 0] = c_in[level - 1]
            return
        moves = [(c_ref.at[level, 1], c_ref.at[level, 0])]
        if level < 3:
            lo, hi = LOHI[2 - level]
            a_ref = as_[level]
            moves.append((a_ref.at[1, pl.ds(lo, hi - lo)], a_ref.at[0, pl.ds(lo, hi - lo)]))
        for k, (src, dst) in enumerate(moves):
            pair_sends.append(
                pltpu.make_async_remote_copy(
                    src_ref=src,
                    dst_ref=dst,
                    send_sem=pair_send_sem.at[level - 1, k],
                    recv_sem=pair_recv_sem.at[level - 1, k],
                    device_id={"gz": inner, "xy": tile},
                    device_id_type=MESH,
                )
            )
            pair_sends[-1].start()

    def from_pair():
        for send in pair_sends:
            send.wait()
        del pair_sends[:]

    acc_ref[...] = jnp.zeros(acc_ref.shape, f32)

    def moments_of(orders):
        def one(p, carry):
            us = []
            for n in orders:
                rhs = lanes_of([c_ref[n, p + 1], c_ref[n, p - 1]])
                u = lax.dot_general(wz_ref[...], rhs, NT, preferred_element_type=f32)
                us.append(u[:128] + u[128:])
            for h in range(2):
                for m in range(3):
                    lv = left_ref[m, pl.ds(2 * z_of(p) + h, 128, stride=8), :]
                    for n, u in zip(orders, us):
                        prod = lv * u[:, 128 * h : 128 * h + 128]
                        tot = prod[0:16]
                        for o in range(1, 8):
                            tot = tot + prod[16 * o : 16 * o + 16]
                        acc_ref[m * 4 + n] += tot
            return carry

        lax.fori_loop(1, 5, one, 0)

    if comm:
        for send in near_sends:
            send.wait()
    else:
        halo_ref[...] = halo_in[...]
    energies(0, [(p, p - 1) for p in range(1, 5)])
    first_rest(((1, 2),))
    to_pair(1)
    first_rest(((2, 2), (3, 2), (4, 2)))
    loads[7].wait()
    moments_of((0,))
    from_pair()
    step(1, ((1, 1), (2, 1), (3, 1)))
    to_pair(2)
    if comm:
        for send in far_sends:
            send.wait()
    energies(1, [(p, 8 - p) for p in range(5, 8)])
    first_rest(((5, 2), (6, 1), (7, 0)))
    step(1, ((4, 1), (5, 1), (6, 0)))
    from_pair()
    step(2, ((1, 0), (2, 0)))
    to_pair(3)
    step(2, ((3, 0), (4, 0), (5, 0)))
    from_pair()
    moments_of((1, 2, 3))
    lanes = iota((8, 128), 1)
    part = jnp.zeros((8, 128), f32)
    for k in range(12):
        tot = jnp.sum(acc_ref[k], axis=1, keepdims=True)
        part = jnp.where(lanes == k, tot[0:8], part)
        part = jnp.where(lanes == k + 16, tot[8:16], part)
    part = part * (2.5 / math.sqrt(8 * 262144))
    part_ref[0] = part

    def send_part(stage, target):
        copies = []
        for step in range(1, 16):
            copy = pltpu.make_async_remote_copy(
                src_ref=part_ref.at[stage],
                dst_ref=got_ref.at[stage, step - 1],
                send_sem=send2_sem.at[stage, step - 1],
                recv_sem=recv2_sem.at[stage, step - 1],
                device_id=target(step),
                device_id_type=MESH,
            )
            copy.start()
            copies.append(copy)
        return copies

    def add_parts(stage, copies, total):
        for copy in copies:
            copy.wait()
        for step in range(1, 16):
            total = total + got_ref[stage, step - 1]
        return total

    if comm:
        copies = send_part(0, along_z)

    def plane_out(p, carry):
        last = f0_ref[p, 0:256].T
        prev = own_rows(f2_ref[p, 80:512], 80).T
        for h in range(2):
            place_of = pl.ds(2 * z_of(p) + h, 128, stride=8)
            last_ref[place_of, :] = last[:, 128 * h : 128 * h + 128]
            prev_ref[place_of, :] = prev[:, 128 * h : 128 * h + 128]
        return carry

    lax.fori_loop(1, 5, plane_out, 0)

    if comm:
        part = add_parts(0, copies, part)
        part_ref[1] = part
        part = add_parts(1, send_part(1, along_plane), part)
    flat = rows([part, jnp.zeros((120, 128), f32)]).T
    for m in range(3):
        moments_ref[m, :, 0:8] = flat[4 * m : 4 * m + 4, 0:8]
        moments_ref[m, :, 8:16] = flat[16 + 4 * m : 20 + 4 * m, 0:8]


def whole(place, comm, *operands):
    hbm = pl.BlockSpec(memory_space=pltpu.HBM)
    vm = pl.BlockSpec(memory_space=pltpu.VMEM)
    plane = lambda kind, lanes: pltpu.VMEM((9, NR, lanes), kind)
    dma = pltpu.SemaphoreType.DMA
    extra = {"collective_id": 0, "has_side_effects": True} if comm else {}
    return pl.pallas_call(
        functools.partial(kernel, place, comm),
        out_shape=(
            jax.ShapeDtypeStruct((3, 4, 16), f32),
            jax.ShapeDtypeStruct((1024, 128), f32),
            jax.ShapeDtypeStruct((1024, 128), f32),
        ),
        in_specs=[hbm] * 8 + [vm] * (len(operands) - 8),
        out_specs=(vm, vm, vm),
        scratch_shapes=[
            pltpu.SMEM((16,), i32),
            pltpu.VMEM((3, 8, 8), f32),
            pltpu.VMEM((8, 8), f32),
            pltpu.VMEM((8, 128), i32),
            pltpu.SMEM((4,), f32),
            pltpu.VMEM((32, 128), i32),
            pltpu.VMEM((32, 128), f32),
            pltpu.VMEM((3, 1024, 128), f32),
            pltpu.VMEM((2, 9, 2, 8, 128), f32),
            pltpu.VMEM((1280, 256), bf16),
            pltpu.VMEM((512, 256), bf16),
            pltpu.VMEM((256, 256), bf16),
            pltpu.VMEM((256, 512), bf16),
            pltpu.VMEM((576, 128), i32),
            pltpu.VMEM((576, 128), f32),
            pltpu.VMEM((9, 576, 128), bf16),
            plane(f32, 128),
            plane(f32, 128),
            plane(f32, 128),
            plane(bf16, 256),
            plane(bf16, 256),
            plane(bf16, 256),
            plane(bf16, 256),
            plane(bf16, 256),
            plane(bf16, 256),
            pltpu.VMEM((4, 6, 256, 256), bf16),
            pltpu.VMEM((528, 384), bf16),
            pltpu.VMEM((480, 16), f32),
            pltpu.VMEM((8, 480, 128), f32),
            pltpu.VMEM((12, 16, 128), f32),
            pltpu.VMEM((2, 8, 128), f32),
            pltpu.VMEM((2, 15, 8, 128), f32),
            dma((8,)),
            dma((17,)),
            dma((17,)),
            dma((3, 2)),
            dma((3, 2)),
            dma((2, 15)),
            dma((2, 15)),
        ],
        compiler_params=pltpu.CompilerParams(vmem_limit_bytes=48 * 1024 * 1024, **extra),
        name="chain",
    )(*[pltpu.with_memory_space_constraint(a, pltpu.HBM) for a in operands[:8]], *operands[8:])


def copy_kernel(a_ref, b_ref, c_ref, a_out, b_out, c_out):
    a_out[...] = a_ref[...]
    b_out[...] = b_ref[...]
    c_out[...] = c_ref[...]


def copied(*arrays):
    spec = pl.BlockSpec(memory_space=pltpu.VMEM)
    return pl.pallas_call(
        copy_kernel,
        out_shape=[jax.ShapeDtypeStruct(a.shape, a.dtype) for a in arrays],
        in_specs=[spec] * 3,
        out_specs=[spec] * 3,
        compiler_params=pltpu.CompilerParams(vmem_limit_bytes=48 * 1024 * 1024),
        name="copied",
    )(*arrays)


def where_am_i():
    tile = lax.axis_index("xy")
    return lax.axis_index("gz"), tile // 8, tile % 8


def per_device(
    left_vectors,
    sign_seeds,
    level_codes,
    level_table,
    disorder_sites,
    disorder_strength,
    hoppings,
    mass_raw,
):
    moments, prev, last = whole(
        where_am_i,
        True,
        sign_seeds,
        hoppings,
        mass_raw,
        level_codes.reshape(8, 128),
        level_table,
        disorder_sites.reshape(32, 128),
        disorder_strength.reshape(32, 128),
        left_vectors.reshape(3, 1024, 128),
    )
    moments, prev, last = copied(moments, prev, last)
    shape = left_vectors.shape[1:]
    return moments, prev.reshape(shape), last.reshape(shape)


def solution(mesh):
    in_specs = (
        P(None, None, None, "gz", "xy", None),
        P(),
        P("gz", "xy", None),
        P(),
        P(),
        P(),
        P(),
        P(),
    )
    out_specs = (P(), P(None, None, "gz", "xy", None), P(None, None, "gz", "xy", None))
    return jax.shard_map(
        per_device, mesh=mesh, in_specs=in_specs, out_specs=out_specs, check_vma=False
    )
```

time: 50.5 us -> 41.8 us (0.83)
  local copies, waits for them, and re-layouts: 5.67 us -> 0 us
  Pallas kernels: 43.9 us -> 41 us
    unnamed x3 -> x0, local copies, waits for them, and re-layouts: 5.67 us -> none
    pallas_call x1, Pallas kernels: 43.9 us -> 39.9 us  [whole(): pl.pallas_call(functools.partial(kernel, place, comm), out_shape=(jax.Sha...]
    pallas_call x0 -> x1, Pallas kernels: none -> 1.04 us  [copied(): pl.pallas_call(copy_kernel, out_shape=[jax.ShapeDtypeStruct(a.shape, a.dt...]
where the time goes in v2:
time: 41.8 us; the launch traced here: 41.6 us
  Pallas kernels  41 us (98%)
  between operations  0.64 us (2%)
    pallas_call x1, Pallas kernels, whole(): pl.pallas_call(functools.partial(kernel, place, comm), out_shape=(jax.Sha...  39.9 us
    pallas_call x1, Pallas kernels, copied(): pl.pallas_call(copy_kernel, out_shape=[jax.ShapeDtypeStruct(a.shape, a.dt...  1.04 us

profile of v2, /device:TPU:1, one launch (start us, length us, event | category | flops | bytes accessed | tf_op | source)
XLA Modules:
  0.0 41.6 jit_solution(13114664032831523888)
XLA Ops:
  0.6 39.9 %chain.1 = (f32[3,4,16]{2,1,0:T(4,128)S(1)}, f32[1024,128]{1,0:T(8,128)S(1)}, f32[1024,128]{1,0:T(8,128)S(1)}) custom-call(s32[16]{0:T(128)} %seed_hbm.1, f32[3,8,8]{2,1,0:T(8,128)} %hop_hbm.1, f32[8,8]{1,0:T(8,128)} %mass_hbm.1, s32[8,128]{1,0:T(8,128)} %bitcast.9, f32[4]{0:T(128)} %table_hbm.1, s32[32,128]{1,0:T(8,128)} %bitcast.7, f32[32,128]{1,0:T(8,128)} %bitcast.8, ...), custom_call_target="tpu_custom_call" | custom-call | tf_op jit(solution)/shard_map/chain/pallas_call | solution.py:547
  40.6 1.0 %copied.1 = (f32[3,4,16]{2,1,0:T(4,128)}, f32[1024,128]{1,0:T(8,128)}, f32[1024,128]{1,0:T(8,128)}) custom-call(f32[3,4,16]{2,1,0:T(4,128)S(1)} %get-tuple-element.9.a_ref, f32[1024,128]{1,0:T(8,128)S(1)} %get-tuple-element.10.b_ref, f32[1024,128]{1,0:T(8,128)S(1)} %get-tuple-element.11.c_ref), custom_call_target="tpu_custom_call" | custom-call | tf_op jit(solution)/shard_map/copied/pallas_call | solution.py:610

commit v3 on v2

--- a/solution.py
+++ b/solution.py
@@ -96,8 +96,7 @@
         wm_ref,
         wy_ref,
         w0_ref,
-        wz_ref,
-        hb_ref,
+            hb_ref,
         mk_ref,
         sb_ref,
         f0_ref,
@@ -110,6 +109,7 @@
         b1_ref,
         b2_ref,
         c_ref,
+        lt_ref,
         sel_ref,
         obc_ref,
         ob_ref,
@@ -136,18 +136,24 @@
         outer = (gz + flip + 4) % 4
         inner = (gz - flip + 4) % 4
         tile = tx * 8 + ty
-        zpos = gz * 4 + tile % 4
         column = tile // 4
 
         def neighbour(dx, dy, z):
             return {"gz": z, "xy": ((tx + dx + 8) % 8) * 8 + (ty + dy + 8) % 8}
 
+        height = gz // 2 * 4 + tile % 4
+        ring = sorted(range(1, 16), key=lambda k: -min(k // 2, 8 - k // 2))
+        square = sorted(range(1, 16), key=lambda k: -min(k // 4, 4 - k // 4) - min(k % 4, 4 - k % 4))
+
         def along_z(step):
-            other = (zpos + step) % 16
-            return {"gz": other // 4, "xy": column * 4 + other % 4}
+            k = ring[step - 1]
+            high = (height + k // 2) % 8
+            return {"gz": high // 4 * 2 + (gz + k) % 2, "xy": column * 4 + high % 4}
 
         def along_plane(step):
-            return {"gz": gz, "xy": ((column + step) % 16) * 4 + tile % 4}
+            k = square[step - 1]
+            y, x = (column // 4 + k // 4) % 4, (column + k) % 4
+            return {"gz": gz, "xy": (y * 4 + x) * 4 + tile % 4}
 
         barrier = pltpu.get_barrier_semaphore()
         partners = [neighbour(dx, dy, outer) for dx, dy in near]
@@ -204,6 +210,102 @@
         block = jnp.where(odd, rows(up), rows(up[::-1]))
         halo_ref[0, 4, h] = rows([block, jnp.zeros((4, 128), f32)])
 
+    for load in loads[4:7]:
+        load.wait()
+    spread = jnp.where(iota((8, 128), 1) >> 4 == iota((8, 128), 0), 1.0, 0.0)
+    mass_raw = mass_ref[...]
+    mats = [0.5 * (mass_raw + mass_raw.T)]
+    for d in range(3):
+        mats += [hop_ref[d].T, hop_ref[d]]
+    wide = jnp.dot(rows(mats) * 0.4, spread, precision=highest, preferred_element_type=f32)
+    wide = [wide[8 * k : 8 * k + 8] for k in range(7)]
+    same_r = (iota((16, 128), 1) & 15) == iota((16, 128), 0)
+
+    def matrix(narrow):
+        blocks = [jnp.where(same_r, jnp.broadcast_to(narrow[b : b + 1], (16, 128)), 0.0) for b in range(8)]
+        return split2(rows(blocks))
+
+    w_mass, w_xp, w_xm, w_yp, w_ym = [matrix(w) for w in wide[:5]]
+    w_next = matrix(jnp.where(odd, wide[5], wide[6]))
+    w_before = matrix(jnp.where(odd, wide[6], wide[5]))
+    for slot, pair in enumerate((w_mass, w_xp, w_xm, w_next, w_before)):
+        both = lanes_of(pair)
+        wm_ref[256 * slot : 256 * slot + 128] = both
+        wm_ref[256 * slot + 128 : 256 * slot + 256] = both
+    for part in range(2):
+        both = lanes_of([w_yp[part], w_ym[part]])
+        wy_ref[256 * part : 256 * part + 128] = both
+        wy_ref[256 * part + 128 : 256 * part + 256] = both
+    w0_ref[0:128] = lanes_of(w_xp)
+    w0_ref[128:256] = -lanes_of(w_xm)
+
+    x, y = rows_to_xy(iota((576, 128), 0) + 8)
+    lane = iota((576, 128), 1)
+    xg = (tx * 16 + x + 128) & 127
+    yg = ty * 16 + y
+    lane1 = iota((1, 128), 1) & 15
+    seeds = jnp.zeros((1, 128), i32)
+    for r in range(16):
+        seeds = jnp.where(lane1 == r, seed_ref[r], seeds)
+    hb_ref[...] = ((xg * 128 + yg) * 8 + (lane >> 4)) * MULT + seeds
+    mk_ref[...] = jnp.where((yg >= 0) & (yg < 128), 1.0, 0.0)
+
+    def sign_plane(p, carry):
+        zg = (gz * 4 + z_of(p) + 16) & 15
+        word = hb_ref[...] + zg * wrap32(128 * 128 * 8 * MULT)
+        word = word ^ lax.shift_right_logical(word, jnp.full(word.shape, 15, i32))
+        word = word * -2048144789
+        word = word ^ lax.shift_right_logical(word, jnp.full(word.shape, 13, i32))
+        word = word * -1028477387
+        mk = mk_ref[...]
+        sb_ref[p] = jnp.where(word < 0, -mk, mk).astype(bf16)
+        return carry
+
+    lax.fori_loop(0, 9, sign_plane, 0)
+
+    at = 0
+    for dx, h, lo, hi in SEGMENTS:
+        xr, yr = rows_to_xy(iota((hi - lo, 128), 0) + lo)
+        xr = xr - 16 * dx - 8 * h
+        ok = (xr >= 0) & (xr < 8)
+        lane = iota((hi - lo, 128), 1)
+        sels = []
+        for dy in (-1, 0, 1):
+            yy = yr - 16 * dy
+            hit = ok & (yy >= 0) & (yy < 16) & (xr * 16 + yy == lane)
+            sels.append(jnp.where(hit, 1.0, 0.0).astype(bf16))
+        sel_ref[at : at + hi - lo] = lanes_of(sels)
+        at += hi - lo
+
+    fs = (f0_ref, f1_ref, f2_ref)
+    as_ = (a0_ref, a1_ref, a2_ref)
+    bs = (b0_ref, b1_ref, b2_ref)
+
+    def keep(level, p, out, lo, hi):
+        hi_f = out.astype(bf16).astype(f32)
+        both = lanes_of([hi_f, out - hi_f])
+        as_[level][p, lo:hi] = both.astype(bf16)
+        bs[level][p, lo - 16 : hi] = rows([both[:8], both, both[:8]]).astype(bf16)
+
+    def start(planes):
+        lhs = []
+        for p, radius in planes:
+            lo, hi = LOHI[radius]
+            lhs.append(lanes_of([sb_ref[p, lo + 16 : hi + 16], sb_ref[p, lo - 32 : hi - 32]]))
+        prod = jnp.dot(rows(lhs), w0_ref[...], preferred_element_type=f32)
+        prod = (prod[:, :128] + prod[:, 128:]) * 2.5
+        at = 0
+        for p, radius in planes:
+            lo, hi = LOHI[radius]
+            out = prod[at : at + hi - lo]
+            at += hi - lo
+            f0_ref[p, lo:hi] = out
+            keep(0, p, out, lo, hi)
+
+    start(((0, 2), (1, 3), (2, 3)))
+    start(((3, 3), (4, 3), (5, 3)))
+    start(((6, 2), (7, 1), (8, 0)))
+
     if comm:
         pl.semaphore_wait(barrier, len(partners))
         near_sends, far_sends = [], []
@@ -221,126 +323,46 @@
             send.start()
             (far_sends if far else near_sends).append(send)
 
-    for load in loads[4:7]:
-        load.wait()
-    spread = jnp.where(iota((8, 128), 1) >> 4 == iota((8, 128), 0), 1.0, 0.0)
-    mass_raw = mass_ref[...]
-    mats = [0.5 * (mass_raw + mass_raw.T)]
-    for d in range(3):
-        mats += [hop_ref[d].T, hop_ref[d]]
-    wide = jnp.dot(rows(mats) * 0.4, spread, precision=highest, preferred_element_type=f32)
-    wide = [wide[8 * k : 8 * k + 8] for k in range(7)]
-    same_r = (iota((16, 128), 1) & 15) == iota((16, 128), 0)
-
-    def matrix(narrow):
-        blocks = [jnp.where(same_r, jnp.broadcast_to(narrow[b : b + 1], (16, 128)), 0.0) for b in range(8)]
-        return split2(rows(blocks))
-
-    w_mass, w_xp, w_xm, w_yp, w_ym = [matrix(w) for w in wide[:5]]
-    w_next = matrix(jnp.where(odd, wide[5], wide[6]))
-    w_before = matrix(jnp.where(odd, wide[6], wide[5]))
-    v_next = matrix(jnp.where(odd, wide[6], -wide[5]))
-    v_before = matrix(jnp.where(odd, -wide[5], wide[6]))
-    for slot, pair in enumerate((w_mass, w_xp, w_xm, w_next, w_before)):
-        both = lanes_of(pair)
-        wm_ref[256 * slot : 256 * slot + 128] = both
-        wm_ref[256 * slot + 128 : 256 * slot + 256] = both
-    for part in range(2):
-        both = lanes_of([w_yp[part], w_ym[part]])
-        wy_ref[256 * part : 256 * part + 128] = both
-        wy_ref[256 * part + 128 : 256 * part + 256] = both
-        wz_ref[128 * part : 128 * part + 128] = lanes_of([v_next[part]] * 2 + [v_before[part]] * 2)
-    w0_ref[0:128] = lanes_of(w_xp)
-    w0_ref[128:256] = -lanes_of(w_xm)
-
-    x, y = rows_to_xy(iota((576, 128), 0) + 8)
-    lane = iota((576, 128), 1)
-    xg = (tx * 16 + x + 128) & 127
-    yg = ty * 16 + y
-    lane1 = iota((1, 128), 1) & 15
-    seeds = jnp.zeros((1, 128), i32)
-    for r in range(16):
-        seeds = jnp.where(lane1 == r, seed_ref[r], seeds)
-    hb_ref[...] = ((xg * 128 + yg) * 8 + (lane >> 4)) * MULT + seeds
-    mk_ref[...] = jnp.where((yg >= 0) & (yg < 128), 1.0, 0.0)
-
-    def sign_plane(p, carry):
-        zg = (gz * 4 + z_of(p) + 16) & 15
-        word = hb_ref[...] + zg * wrap32(128 * 128 * 8 * MULT)
-        word = word ^ lax.shift_right_logical(word, jnp.full(word.shape, 15, i32))
-        word = word * -2048144789
-        word = word ^ lax.shift_right_logical(word, jnp.full(word.shape, 13, i32))
-        word = word * -1028477387
-        mk = mk_ref[...]
-        sb_ref[p] = jnp.where(word < 0, -mk, mk).astype(bf16)
+    loads[7].wait()
+
+    def turn_left(p, carry):
+        for m in range(3):
+            for h in range(2):
+                lt_ref[m, p - 1, 128 * h : 128 * h + 128] = left_ref[m, pl.ds(2 * z_of(p) + h, 128, stride=8), :].T
         return carry
 
-    lax.fori_loop(0, 9, sign_plane, 0)
-
-    at = 0
-    for dx, h, lo, hi in SEGMENTS:
-        xr, yr = rows_to_xy(iota((hi - lo, 128), 0) + lo)
-        xr = xr - 16 * dx - 8 * h
-        ok = (xr >= 0) & (xr < 8)
-        lane = iota((hi - lo, 128), 1)
-        sels = []
-        for dy in (-1, 0, 1):
-            yy = yr - 16 * dy
-            hit = ok & (yy >= 0) & (yy < 16) & (xr * 16 + yy == lane)
-            sels.append(jnp.where(hit, 1.0, 0.0).astype(bf16))
-        sel_ref[at : at + hi - lo] = lanes_of(sels)
-        at += hi - lo
-
-    fs = (f0_ref, f1_ref, f2_ref)
-    as_ = (a0_ref, a1_ref, a2_ref)
-    bs = (b0_ref, b1_ref, b2_ref)
-
-    def keep(level, p, out, lo, hi):
-        hi_f = out.astype(bf16).astype(f32)
-        both = lanes_of([hi_f, out - hi_f])
-        as_[level][p, lo:hi] = both.astype(bf16)
-        bs[level][p, lo - 16 : hi] = rows([both[:8], both, both[:8]]).astype(bf16)
-        if p <= 5:
-            c_ref[level, p] = own_rows(both, lo).astype(bf16)
-
-    def start(planes):
-        lhs = []
+    lax.fori_loop(1, 5, turn_left, 0)
+    acc_ref[...] = jnp.zeros(acc_ref.shape, f32)
+
+    def halves(both):
+        return both[:, :128] + both[:, 128:]
+
+    def add_moments(n, p, velocity):
+        for m in range(3):
+            prod = lt_ref[m, p - 1] * velocity
+            tot = prod[0:8]
+            for k in range(8, 256, 8):
+                tot = tot + prod[k : k + 8]
+            acc_ref[m * 4 + n] += tot
+
+    def hop(n, planes):
+        a_ref, b_ref = as_[n], bs[n]
+        lhs, nxt, before, ylhs = [], [], [], []
         for p, radius in planes:
             lo, hi = LOHI[radius]
-            lhs.append(lanes_of([sb_ref[p, lo + 16 : hi + 16], sb_ref[p, lo - 32 : hi - 32]]))
-        prod = jnp.dot(rows(lhs), w0_ref[...], preferred_element_type=f32)
-        prod = (prod[:, :128] + prod[:, 128:]) * 2.5
-        at = 0
-        for p, radius in planes:
-            lo, hi = LOHI[radius]
-            out = prod[at : at + hi - lo]
-            at += hi - lo
-            f0_ref[p, lo:hi] = out
-            keep(0, p, out, lo, hi)
-
-    start(((0, 2), (1, 3), (2, 3)))
-    start(((3, 3), (4, 3), (5, 3)))
-    start(((6, 2), (7, 1), (8, 0)))
-
-    def hop(n, planes):
-        a_ref, b_ref = as_[n], bs[n]
-        lhs, ylhs = [], []
-        for p, radius in planes:
-            lo, hi = LOHI[radius]
-            lhs.append(
-                lanes_of(
-                    [
-                        a_ref[p, lo:hi],
-                        b_ref[p, lo + 16 : hi + 16],
-                        b_ref[p, lo - 32 : hi - 32],
-                        a_ref[p + 1, lo:hi],
-                        a_ref[p - 1, lo:hi],
-                    ]
-                )
-            )
+            lhs.append(lanes_of([a_ref[p, lo:hi], b_ref[p, lo + 16 : hi + 16], b_ref[p, lo - 32 : hi - 32]]))
+            nxt.append(a_ref[p + 1, lo:hi])
+            before.append(a_ref[p - 1, lo:hi])
             first = 0 if radius == 1 else 16
             ylhs.append(a_ref[p, lo - first : hi + 16 - first])
-        main = jnp.dot(rows(lhs), wm_ref[...], preferred_element_type=f32)
+        own = planes[0][0] <= 4
+        if own:
+            main = halves(jnp.dot(rows(lhs), wm_ref[0:768], preferred_element_type=f32))
+            nxt = halves(jnp.dot(rows(nxt), wm_ref[768:1024], preferred_element_type=f32))
+            before = halves(jnp.dot(rows(before), wm_ref[1024:1280], preferred_element_type=f32))
+        else:
+            all_lhs = lanes_of([rows(lhs), rows(nxt), rows(before)])
+            main = halves(jnp.dot(all_lhs, wm_ref[...], preferred_element_type=f32))
         ylhs = rows(ylhs)
         yy = jnp.dot(lanes_of([ylhs, ylhs]), wy_ref[...], preferred_element_type=f32)
         yp = pltpu.roll(yy[:, :128], yy.shape[0] - 1, 0)
@@ -350,7 +372,13 @@
             lo, hi = LOHI[radius]
             first = 0 if radius == 1 else 16
             size, t = hi - lo, s + first
-            outs.append(main[r : r + size, :128] + main[r : r + size, 128:] + yp[t : t + size] + ym[t : t + size])
+            out = main[r : r + size] + yp[t : t + size] + ym[t : t + size]
+            if own:
+                up, down = nxt[r : r + size], before[r : r + size]
+                out = out + up + down
+                if p <= 4:
+                    add_moments(n, p, own_rows(up, lo) - own_rows(down, lo))
+            outs.append(out)
             r += size
             s += size + 16
         return outs
@@ -360,8 +388,8 @@
             lo, hi = LOHI[radius]
             f1_ref[p, lo:hi] = out
 
-    first_hop(((1, 2), (2, 2), (3, 2)))
-    first_hop(((4, 2), (5, 2), (6, 1), (7, 0)))
+    first_hop(((1, 2), (2, 2), (3, 2), (4, 2)))
+    first_hop(((5, 2), (6, 1), (7, 0)))
 
     def energies(far, planes):
         obc_ref[...] = jnp.zeros(obc_ref.shape, f32)
@@ -401,7 +429,7 @@
             else:
                 v = own_rows(out, lo)
                 hi_f = v.astype(bf16).astype(f32)
-                c_ref[3, p] = lanes_of([hi_f, v - hi_f]).astype(bf16)
+                c_ref[p] = lanes_of([hi_f, v - hi_f]).astype(bf16)
                 f0_ref[p, 0:256] = v
 
     pair_sends = []
@@ -410,52 +438,30 @@
         if not comm:
             if level < 3:
                 as_[level][0] = (a1_in, a2_in)[level - 1][...]
-            c_ref[level, 0] = c_in[level - 1]
+            else:
+                c_ref[0] = c_in[2]
             return
-        moves = [(c_ref.at[level, 1], c_ref.at[level, 0])]
         if level < 3:
             lo, hi = LOHI[2 - level]
-            a_ref = as_[level]
-            moves.append((a_ref.at[1, pl.ds(lo, hi - lo)], a_ref.at[0, pl.ds(lo, hi - lo)]))
-        for k, (src, dst) in enumerate(moves):
-            pair_sends.append(
-                pltpu.make_async_remote_copy(
-                    src_ref=src,
-                    dst_ref=dst,
-                    send_sem=pair_send_sem.at[level - 1, k],
-                    recv_sem=pair_recv_sem.at[level - 1, k],
-                    device_id={"gz": inner, "xy": tile},
-                    device_id_type=MESH,
-                )
+            face = as_[level].at[:, pl.ds(lo, hi - lo)]
+        else:
+            face = c_ref
+        pair_sends.append(
+            pltpu.make_async_remote_copy(
+                src_ref=face.at[1],
+                dst_ref=face.at[0],
+                send_sem=pair_send_sem.at[level - 1],
+                recv_sem=pair_recv_sem.at[level - 1],
+                device_id={"gz": inner, "xy": tile},
+                device_id_type=MESH,
             )
-            pair_sends[-1].start()
+        )
+        pair_sends[-1].start()
 
     def from_pair():
         for send in pair_sends:
             send.wait()
         del pair_sends[:]
-
-    acc_ref[...] = jnp.zeros(acc_ref.shape, f32)
-
-    def moments_of(orders):
-        def one(p, carry):
-            us = []
-            for n in orders:
-                rhs = lanes_of([c_ref[n, p + 1], c_ref[n, p - 1]])
-                u = lax.dot_general(wz_ref[...], rhs, NT, preferred_element_type=f32)
-                us.append(u[:128] + u[128:])
-            for h in range(2):
-                for m in range(3):
-                    lv = left_ref[m, pl.ds(2 * z_of(p) + h, 128, stride=8), :]
-                    for n, u in zip(orders, us):
-                        prod = lv * u[:, 128 * h : 128 * h + 128]
-                        tot = prod[0:16]
-                        for o in range(1, 8):
-                            tot = tot + prod[16 * o : 16 * o + 16]
-                        acc_ref[m * 4 + n] += tot
-            return carry
-
-        lax.fori_loop(1, 5, one, 0)
 
     if comm:
         for send in near_sends:
@@ -466,10 +472,9 @@
     first_rest(((1, 2),))
     to_pair(1)
     first_rest(((2, 2), (3, 2), (4, 2)))
-    loads[7].wait()
-    moments_of((0,))
+    step(1, ((2, 1), (3, 1)))
     from_pair()
-    step(1, ((1, 1), (2, 1), (3, 1)))
+    step(1, ((1, 1),))
     to_pair(2)
     if comm:
         for send in far_sends:
@@ -481,15 +486,23 @@
     step(2, ((1, 0), (2, 0)))
     to_pair(3)
     step(2, ((3, 0), (4, 0), (5, 0)))
+
+    def z_product(slot, planes):
+        lhs = rows([c_ref[p] for p in planes])
+        return halves(jnp.dot(lhs, wm_ref[256 * slot : 256 * slot + 256], preferred_element_type=f32))
+
+    nxt = z_product(3, (2, 3, 4, 5))
+    before = z_product(4, (1, 2, 3))
+    for p in (2, 3, 4):
+        add_moments(3, p, nxt[256 * p - 256 : 256 * p] - before[256 * p - 512 : 256 * p - 256])
     from_pair()
-    moments_of((1, 2, 3))
-    lanes = iota((8, 128), 1)
-    part = jnp.zeros((8, 128), f32)
-    for k in range(12):
-        tot = jnp.sum(acc_ref[k], axis=1, keepdims=True)
-        part = jnp.where(lanes == k, tot[0:8], part)
-        part = jnp.where(lanes == k + 16, tot[8:16], part)
-    part = part * (2.5 / math.sqrt(8 * 262144))
+    add_moments(3, 1, nxt[:256] - z_product(4, (0,)))
+
+    fold = jnp.where((iota((128, 128), 0) & 15) == (iota((128, 128), 1) & 15), 1.0, 0.0)
+    folded = jnp.dot(acc_ref[...].reshape(96, 128), fold, precision=highest, preferred_element_type=f32)
+    mine = (iota((96, 128), 1) >> 4) == ((iota((96, 128), 0) >> 3) & 7)
+    folded = jnp.where(mine, folded, 0.0) * (flip.astype(f32) * (2.5 / math.sqrt(8 * 262144)))
+    part = rows([jnp.sum(folded[:64], axis=0, keepdims=True), jnp.sum(folded[64:], axis=0, keepdims=True)])
     part_ref[0] = part
 
     def send_part(stage, target):
@@ -532,10 +545,8 @@
         part = add_parts(0, copies, part)
         part_ref[1] = part
         part = add_parts(1, send_part(1, along_plane), part)
-    flat = rows([part, jnp.zeros((120, 128), f32)]).T
-    for m in range(3):
-        moments_ref[m, :, 0:8] = flat[4 * m : 4 * m + 4, 0:8]
-        moments_ref[m, :, 8:16] = flat[16 + 4 * m : 20 + 4 * m, 0:8]
+    for k in range(12):
+        moments_ref[k // 4, k % 4 : k % 4 + 1, :] = part[k // 8 : k // 8 + 1, 16 * (k % 8) : 16 * (k % 8) + 16]
 
 
 def whole(place, comm, *operands):
@@ -566,7 +577,6 @@
             pltpu.VMEM((1280, 256), bf16),
             pltpu.VMEM((512, 256), bf16),
             pltpu.VMEM((256, 256), bf16),
-            pltpu.VMEM((256, 512), bf16),
             pltpu.VMEM((576, 128), i32),
             pltpu.VMEM((576, 128), f32),
             pltpu.VMEM((9, 576, 128), bf16),
@@ -579,18 +589,19 @@
             plane(bf16, 256),
             plane(bf16, 256),
             plane(bf16, 256),
-            pltpu.VMEM((4, 6, 256, 256), bf16),
+            pltpu.VMEM((6, 256, 256), bf16),
+            pltpu.VMEM((3, 4, 256, 128), f32),
             pltpu.VMEM((528, 384), bf16),
             pltpu.VMEM((480, 16), f32),
             pltpu.VMEM((8, 480, 128), f32),
-            pltpu.VMEM((12, 16, 128), f32),
-            pltpu.VMEM((2, 8, 128), f32),
-            pltpu.VMEM((2, 15, 8, 128), f32),
+            pltpu.VMEM((12, 8, 128), f32),
+            pltpu.VMEM((2, 2, 128), f32),
+            pltpu.VMEM((2, 15, 2, 128), f32),
             dma((8,)),
             dma((17,)),
             dma((17,)),
-            dma((3, 2)),
-            dma((3, 2)),
+            dma((3,)),
+            dma((3,)),
             dma((2, 15)),
             dma((2, 15)),
         ],

time: 41.8 us -> 38.9 us (0.931)
  Pallas kernels: 41 us -> 38.1 us
    pallas_call x1, Pallas kernels: 39.9 us -> 37.1 us  [whole(): pl.pallas_call(functools.partial(kernel, place, comm), out_shape=(jax.Sha...]
where the time goes in v3:
time: 38.9 us; the launch traced here: 38.7 us
  Pallas kernels  38.1 us (98%)
  between operations  0.64 us (2%)
    pallas_call x1, Pallas kernels, whole(): pl.pallas_call(functools.partial(kernel, place, comm), out_shape=(jax.Sha...  37.1 us
    pallas_call x1, Pallas kernels, copied(): pl.pallas_call(copy_kernel, out_shape=[jax.ShapeDtypeStruct(a.shape, a.dt...  1.04 us

profile of v3, /device:TPU:1, one launch (start us, length us, event | category | flops | bytes accessed | tf_op | source)
XLA Modules:
  0.0 38.7 jit_solution(9769603439506419216)
XLA Ops:
  0.6 37.1 %chain.1 = (f32[3,4,16]{2,1,0:T(4,128)S(1)}, f32[1024,128]{1,0:T(8,128)S(1)}, f32[1024,128]{1,0:T(8,128)S(1)}) custom-call(s32[16]{0:T(128)} %seed_hbm.1, f32[3,8,8]{2,1,0:T(8,128)} %hop_hbm.1, f32[8,8]{1,0:T(8,128)} %mass_hbm.1, s32[8,128]{1,0:T(8,128)} %bitcast.9, f32[4]{0:T(128)} %table_hbm.1, s32[32,128]{1,0:T(8,128)} %bitcast.7, f32[32,128]{1,0:T(8,128)} %bitcast.8, ...), custom_call_target="tpu_custom_call" | custom-call | tf_op jit(solution)/shard_map/chain/pallas_call | solution.py:558
  37.7 1.0 %copied.1 = (f32[3,4,16]{2,1,0:T(4,128)}, f32[1024,128]{1,0:T(8,128)}, f32[1024,128]{1,0:T(8,128)}) custom-call(f32[3,4,16]{2,1,0:T(4,128)S(1)} %get-tuple-element.9.a_ref, f32[1024,128]{1,0:T(8,128)S(1)} %get-tuple-element.10.b_ref, f32[1024,128]{1,0:T(8,128)S(1)} %get-tuple-element.11.c_ref), custom_call_target="tpu_custom_call" | custom-call | tf_op jit(solution)/shard_map/copied/pallas_call | solution.py:621

commit v4 on v3

--- a/solution.py
+++ b/solution.py
@@ -131,6 +131,9 @@
     def z_of(p):
         return (3 * (1 - gz % 2)) + flip * (p - 1)
 
+    def await_copies(whole_ref, sem):
+        pltpu.make_async_copy(whole_ref, whole_ref, sem).wait()
+
     if comm:
         near = [(dx, dy) for dx in (-1, 0, 1) for dy in (-1, 0, 1) if (dx, dy) != (0, 0)]
         outer = (gz + flip + 4) % 4
@@ -208,7 +211,7 @@
     for h in range(2):
         up = [onsite[2 * z + h : 2 * z + h + 1] for z in range(4)]
         block = jnp.where(odd, rows(up), rows(up[::-1]))
-        halo_ref[0, 4, h] = rows([block, jnp.zeros((4, 128), f32)])
+        halo_ref[0, 8 + h] = block
 
     for load in loads[4:7]:
         load.wait()
@@ -303,25 +306,24 @@
             keep(0, p, out, lo, hi)
 
     start(((0, 2), (1, 3), (2, 3)))
+    if comm:
+        pl.semaphore_wait(barrier, len(partners))
+        for dx, dy, far in (
+            [(dx, dy, True) for dx, dy in near] + [(0, 0, True)] + [(dx, dy, False) for dx, dy in near]
+        ):
+            first, count = (1 if dx > 0 else 0, 1) if dx else (0, 2)
+            there = 2 * ((1 - dx) * 3 + 1 - dy) + first
+            pltpu.make_async_remote_copy(
+                src_ref=halo_ref.at[0, pl.ds(8 + first, count)],
+                dst_ref=halo_ref.at[int(far), pl.ds(there, count)],
+                send_sem=send_sem,
+                recv_sem=recv_sem.at[int(far)],
+                device_id=neighbour(dx, dy, outer if far else gz),
+                device_id_type=MESH,
+            ).start()
+
     start(((3, 3), (4, 3), (5, 3)))
     start(((6, 2), (7, 1), (8, 0)))
-
-    if comm:
-        pl.semaphore_wait(barrier, len(partners))
-        near_sends, far_sends = [], []
-        for k, (dx, dy, far) in enumerate(
-            [(dx, dy, True) for dx, dy in near] + [(0, 0, True)] + [(dx, dy, False) for dx, dy in near]
-        ):
-            send = pltpu.make_async_remote_copy(
-                src_ref=halo_ref.at[0, 4],
-                dst_ref=halo_ref.at[int(far), (1 - dx) * 3 + 1 - dy],
-                send_sem=send_sem.at[k],
-                recv_sem=recv_sem.at[k],
-                device_id=neighbour(dx, dy, outer if far else gz),
-                device_id_type=MESH,
-            )
-            send.start()
-            (far_sends if far else near_sends).append(send)
 
     loads[7].wait()
 
@@ -398,8 +400,8 @@
             sels, vals = [], []
             for dy in (-1, 0, 1):
                 sel = sel_ref[at : at + hi - lo, 128 * (dy + 1) : 128 * (dy + 2)]
-                block = halo_ref[far, (dx + 1) * 3 + dy + 1, h]
-                for piece in split3(rows([block, jnp.zeros((8, 128), f32)])):
+                block = halo_ref[far, 2 * ((dx + 1) * 3 + dy + 1) + h]
+                for piece in split3(rows([block, jnp.zeros((12, 128), f32)])):
                     sels.append(sel)
                     vals.append(piece)
             at += hi - lo
@@ -464,8 +466,7 @@
         del pair_sends[:]
 
     if comm:
-        for send in near_sends:
-            send.wait()
+        await_copies(halo_ref.at[0, pl.ds(0, 10)], recv_sem.at[0])
     else:
         halo_ref[...] = halo_in[...]
     energies(0, [(p, p - 1) for p in range(1, 5)])
@@ -477,8 +478,7 @@
     step(1, ((1, 1),))
     to_pair(2)
     if comm:
-        for send in far_sends:
-            send.wait()
+        await_copies(halo_ref.at[1, pl.ds(0, 12)], recv_sem.at[1])
     energies(1, [(p, 8 - p) for p in range(5, 8)])
     first_rest(((5, 2), (6, 1), (7, 0)))
     step(1, ((4, 1), (5, 1), (6, 0)))
@@ -506,29 +506,22 @@
     part_ref[0] = part
 
     def send_part(stage, target):
-        copies = []
         for step in range(1, 16):
-            copy = pltpu.make_async_remote_copy(
+            pltpu.make_async_remote_copy(
                 src_ref=part_ref.at[stage],
                 dst_ref=got_ref.at[stage, step - 1],
-                send_sem=send2_sem.at[stage, step - 1],
-                recv_sem=recv2_sem.at[stage, step - 1],
+                send_sem=send2_sem.at[stage],
+                recv_sem=recv2_sem.at[stage],
                 device_id=target(step),
                 device_id_type=MESH,
-            )
-            copy.start()
-            copies.append(copy)
-        return copies
-
-    def add_parts(stage, copies, total):
-        for copy in copies:
-            copy.wait()
-        for step in range(1, 16):
-            total = total + got_ref[stage, step - 1]
-        return total
+            ).start()
+
+    def add_parts(stage, total):
+        await_copies(got_ref.at[stage], recv2_sem.at[stage])
+        return total + jnp.sum(got_ref[stage], axis=0)
 
     if comm:
-        copies = send_part(0, along_z)
+        send_part(0, along_z)
 
     def plane_out(p, carry):
         last = f0_ref[p, 0:256].T
@@ -542,9 +535,14 @@
     lax.fori_loop(1, 5, plane_out, 0)
 
     if comm:
-        part = add_parts(0, copies, part)
+        part = add_parts(0, part)
         part_ref[1] = part
-        part = add_parts(1, send_part(1, along_plane), part)
+        send_part(1, along_plane)
+        part = add_parts(1, part)
+        await_copies(halo_ref.at[0, pl.ds(0, 10)], send_sem)
+        await_copies(halo_ref.at[1, pl.ds(0, 12)], send_sem)
+        await_copies(got_ref.at[0], send2_sem.at[0])
+        await_copies(got_ref.at[1], send2_sem.at[1])
     for k in range(12):
         moments_ref[k // 4, k % 4 : k % 4 + 1, :] = part[k // 8 : k // 8 + 1, 16 * (k % 8) : 16 * (k % 8) + 16]
 
@@ -573,7 +571,7 @@
             pltpu.VMEM((32, 128), i32),
             pltpu.VMEM((32, 128), f32),
             pltpu.VMEM((3, 1024, 128), f32),
-            pltpu.VMEM((2, 9, 2, 8, 128), f32),
+            pltpu.VMEM((2, 18, 4, 128), f32),
             pltpu.VMEM((1280, 256), bf16),
             pltpu.VMEM((512, 256), bf16),
             pltpu.VMEM((256, 256), bf16),
@@ -598,31 +596,34 @@
             pltpu.VMEM((2, 2, 128), f32),
             pltpu.VMEM((2, 15, 2, 128), f32),
             dma((8,)),
-            dma((17,)),
-            dma((17,)),
+            dma,
+            dma((2,)),
             dma((3,)),
             dma((3,)),
-            dma((2, 15)),
-            dma((2, 15)),
+            dma((2,)),
+            dma((2,)),
         ],
         compiler_params=pltpu.CompilerParams(vmem_limit_bytes=48 * 1024 * 1024, **extra),
         name="chain",
     )(*[pltpu.with_memory_space_constraint(a, pltpu.HBM) for a in operands[:8]], *operands[8:])
 
 
-def copy_kernel(a_ref, b_ref, c_ref, a_out, b_out, c_out):
-    a_out[...] = a_ref[...]
-    b_out[...] = b_ref[...]
-    c_out[...] = c_ref[...]
+def copy_kernel(a_ref, b_ref, c_ref, a_out, b_out, c_out, sems):
+    copies = []
+    for k, (src, dst) in enumerate(((b_ref, b_out), (c_ref, c_out), (a_ref, a_out))):
+        copies.append(pltpu.make_async_copy(src, dst, sems.at[k]))
+        copies[-1].start()
+    for copy in copies:
+        copy.wait()
 
 
 def copied(*arrays):
-    spec = pl.BlockSpec(memory_space=pltpu.VMEM)
     return pl.pallas_call(
         copy_kernel,
         out_shape=[jax.ShapeDtypeStruct(a.shape, a.dtype) for a in arrays],
-        in_specs=[spec] * 3,
-        out_specs=[spec] * 3,
+        in_specs=[pl.BlockSpec(memory_space=pltpu.VMEM)] * 3,
+        out_specs=[pl.BlockSpec(memory_space=pltpu.HBM)] * 3,
+        scratch_shapes=[pltpu.SemaphoreType.DMA((3,))],
         compiler_params=pltpu.CompilerParams(vmem_limit_bytes=48 * 1024 * 1024),
         name="copied",
     )(*arrays)

time: 38.9 us -> 36.5 us (0.938)
  Pallas kernels: 38.1 us -> 35.7 us
    pallas_call x1, Pallas kernels: 37.1 us -> 34.7 us  [whole(): pl.pallas_call(functools.partial(kernel, place, comm), out_shape=(jax.Sha...]
where the time goes in v4:
time: 36.5 us; the launch traced here: 36.3 us
  Pallas kernels  35.7 us (98%)
  between operations  0.64 us (2%)
    pallas_call x1, Pallas kernels, whole(): pl.pallas_call(functools.partial(kernel, place, comm), out_shape=(jax.Sha...  34.7 us
    pallas_call x1, Pallas kernels, copied(): pl.pallas_call(copy_kernel, out_shape=[jax.ShapeDtypeStruct(a.shape, a.dt...  1 us

profile of v4, /device:TPU:1, one launch (start us, length us, event | category | flops | bytes accessed | tf_op | source)
XLA Modules:
  0.0 36.3 jit_solution(14478176595291188157)
XLA Ops:
  0.6 34.7 %chain.1 = (f32[3,4,16]{2,1,0:T(4,128)S(1)}, f32[1024,128]{1,0:T(8,128)S(1)}, f32[1024,128]{1,0:T(8,128)S(1)}) custom-call(s32[16]{0:T(128)} %seed_hbm.1, f32[3,8,8]{2,1,0:T(8,128)} %hop_hbm.1, f32[8,8]{1,0:T(8,128)} %mass_hbm.1, s32[8,128]{1,0:T(8,128)} %bitcast.9, f32[4]{0:T(128)} %table_hbm.1, s32[32,128]{1,0:T(8,128)} %bitcast.7, f32[32,128]{1,0:T(8,128)} %bitcast.8, ...), custom_call_target="tpu_custom_call" | custom-call | tf_op jit(solution)/shard_map/chain/pallas_call | solution.py:556
  35.3 1.0 %copied.1 = (f32[3,4,16]{2,1,0:T(4,128)}, f32[1024,128]{1,0:T(8,128)}, f32[1024,128]{1,0:T(8,128)}) custom-call(f32[3,4,16]{2,1,0:T(4,128)S(1)} %get-tuple-element.9.a_ref, f32[1024,128]{1,0:T(8,128)S(1)} %get-tuple-element.10.b_ref, f32[1024,128]{1,0:T(8,128)S(1)} %get-tuple-element.11.c_ref), custom_call_target="tpu_custom_call" | custom-call | tf_op jit(solution)/shard_map/copied/pallas_call | solution.py:621

commit v5 on v4

--- a/solution.py
+++ b/solution.py
@@ -408,6 +408,9 @@
             obc_ref[lo - 64 : hi - 64] += lax.dot_general(
                 lanes_of(sels), lanes_of(vals), NT, preferred_element_type=f32
             )
+        spread_energies(planes)
+
+    def spread_energies(planes):
         for p, col in planes:
             ob_ref[p] = jnp.broadcast_to(obc_ref[:, col : col + 1] * 0.4, (480, 128))
 
@@ -469,9 +472,10 @@
         await_copies(halo_ref.at[0, pl.ds(0, 10)], recv_sem.at[0])
     else:
         halo_ref[...] = halo_in[...]
-    energies(0, [(p, p - 1) for p in range(1, 5)])
+    energies(0, [(1, 0)])
     first_rest(((1, 2),))
     to_pair(1)
+    spread_energies([(p, p - 1) for p in range(2, 5)])
     first_rest(((2, 2), (3, 2), (4, 2)))
     step(1, ((2, 1), (3, 1)))
     from_pair()
@@ -482,10 +486,11 @@
     energies(1, [(p, 8 - p) for p in range(5, 8)])
     first_rest(((5, 2), (6, 1), (7, 0)))
     step(1, ((4, 1), (5, 1), (6, 0)))
+    step(2, ((2, 0), (3, 0)))
     from_pair()
-    step(2, ((1, 0), (2, 0)))
+    step(2, ((1, 0),))
     to_pair(3)
-    step(2, ((3, 0), (4, 0), (5, 0)))
+    step(2, ((4, 0), (5, 0)))
 
     def z_product(slot, planes):
         lhs = rows([c_ref[p] for p in planes])

time: 36.5 us -> 36 us (0.986)
  Pallas kernels: 35.7 us -> 35.2 us
    pallas_call x1, Pallas kernels: 34.7 us -> 34.3 us  [whole(): pl.pallas_call(functools.partial(kernel, place, comm), out_shape=(jax.Sha...]
where the time goes in v5:
time: 36 us; the launch traced here: 35.9 us
  Pallas kernels  35.2 us (98%)
  between operations  0.64 us (2%)
    pallas_call x1, Pallas kernels, whole(): pl.pallas_call(functools.partial(kernel, place, comm), out_shape=(jax.Sha...  34.3 us
    pallas_call x1, Pallas kernels, copied(): pl.pallas_call(copy_kernel, out_shape=[jax.ShapeDtypeStruct(a.shape, a.dt...  1 us

profile of v5, /device:TPU:1, one launch (start us, length us, event | category | flops | bytes accessed | tf_op | source)
XLA Modules:
  0.0 35.9 jit_solution(7232525433889730467)
XLA Ops:
  0.6 34.3 %chain.1 = (f32[3,4,16]{2,1,0:T(4,128)S(1)}, f32[1024,128]{1,0:T(8,128)S(1)}, f32[1024,128]{1,0:T(8,128)S(1)}) custom-call(s32[16]{0:T(128)} %seed_hbm.1, f32[3,8,8]{2,1,0:T(8,128)} %hop_hbm.1, f32[8,8]{1,0:T(8,128)} %mass_hbm.1, s32[8,128]{1,0:T(8,128)} %bitcast.9, f32[4]{0:T(128)} %table_hbm.1, s32[32,128]{1,0:T(8,128)} %bitcast.7, f32[32,128]{1,0:T(8,128)} %bitcast.8, ...), custom_call_target="tpu_custom_call" | custom-call | tf_op jit(solution)/shard_map/chain/pallas_call | solution.py:561
  34.9 1.0 %copied.1 = (f32[3,4,16]{2,1,0:T(4,128)}, f32[1024,128]{1,0:T(8,128)}, f32[1024,128]{1,0:T(8,128)}) custom-call(f32[3,4,16]{2,1,0:T(4,128)S(1)} %get-tuple-element.9.a_ref, f32[1024,128]{1,0:T(8,128)S(1)} %get-tuple-element.10.b_ref, f32[1024,128]{1,0:T(8,128)S(1)} %get-tuple-element.11.c_ref), custom_call_target="tpu_custom_call" | custom-call | tf_op jit(solution)/shard_map/copied/pallas_call | solution.py:626

commit v6 on v5

--- a/solution.py
+++ b/solution.py
@@ -309,7 +309,7 @@
     if comm:
         pl.semaphore_wait(barrier, len(partners))
         for dx, dy, far in (
-            [(dx, dy, True) for dx, dy in near] + [(0, 0, True)] + [(dx, dy, False) for dx, dy in near]
+            [(dx, dy, False) for dx, dy in near] + [(dx, dy, True) for dx, dy in near] + [(0, 0, True)]
         ):
             first, count = (1 if dx > 0 else 0, 1) if dx else (0, 2)
             there = 2 * ((1 - dx) * 3 + 1 - dy) + first

time: 36 us -> 36 us (level)
  no operation moved by 1% of the time
where the time goes in v6:
time: 36 us; the launch traced here: 35.8 us
  Pallas kernels  35.2 us (98%)
  between operations  0.64 us (2%)
    pallas_call x1, Pallas kernels, whole(): pl.pallas_call(functools.partial(kernel, place, comm), out_shape=(jax.Sha...  34.2 us
    pallas_call x1, Pallas kernels, copied(): pl.pallas_call(copy_kernel, out_shape=[jax.ShapeDtypeStruct(a.shape, a.dt...  1 us

profile of v6, /device:TPU:1, one launch (start us, length us, event | category | flops | bytes accessed | tf_op | source)
XLA Modules:
  0.0 35.8 jit_solution(6460612370023238792)
XLA Ops:
  0.6 34.2 %chain.1 = (f32[3,4,16]{2,1,0:T(4,128)S(1)}, f32[1024,128]{1,0:T(8,128)S(1)}, f32[1024,128]{1,0:T(8,128)S(1)}) custom-call(s32[16]{0:T(128)} %seed_hbm.1, f32[3,8,8]{2,1,0:T(8,128)} %hop_hbm.1, f32[8,8]{1,0:T(8,128)} %mass_hbm.1, s32[8,128]{1,0:T(8,128)} %bitcast.9, f32[4]{0:T(128)} %table_hbm.1, s32[32,128]{1,0:T(8,128)} %bitcast.7, f32[32,128]{1,0:T(8,128)} %bitcast.8, ...), custom_call_target="tpu_custom_call" | custom-call | tf_op jit(solution)/shard_map/chain/pallas_call | solution.py:561
  34.8 1.0 %copied.1 = (f32[3,4,16]{2,1,0:T(4,128)}, f32[1024,128]{1,0:T(8,128)}, f32[1024,128]{1,0:T(8,128)}) custom-call(f32[3,4,16]{2,1,0:T(4,128)S(1)} %get-tuple-element.9.a_ref, f32[1024,128]{1,0:T(8,128)S(1)} %get-tuple-element.10.b_ref, f32[1024,128]{1,0:T(8,128)S(1)} %get-tuple-element.11.c_ref), custom_call_target="tpu_custom_call" | custom-call | tf_op jit(solution)/shard_map/copied/pallas_call | solution.py:626
